TPU v7x, 256 devices: a whole 4x4x8 slice. The times are simulated.
256 devices in a mesh: space: 64 (over x, z, core), tm: 4 (over y).
Axes of the slice: x: 4, y: 4, z: 8, core: 2. Of those that a mesh axis runs over, the one named last changes fastest.
Arguments:
- queries: bfloat16 [4, 16384, 1024], P('tm', 'space'), may hold values from -6 to 6
- key_vectors: bfloat16 [4, 16384, 1024], P('tm', 'space'), may hold values from -6 to 6
- value_vectors: bfloat16 [4, 16384, 1024], P('tm', 'space'), may hold values from -6 to 6
- query_time: bfloat16 [4, 16384, 1024], P('tm', 'space'), may hold values from -6 to 6
- key_time: bfloat16 [4, 16384, 1024], P('tm', 'space'), may hold values from -6 to 6
- out_grad: bfloat16 [4, 16384, 1024], P('tm', 'space'), may hold values from -6 to 6
- fluid_mask: int32 [128], replicated, may hold values from 0 to 1, as said below
- occupancy: int32 [16384], replicated, may hold values 0 or 1
- key_lists: int32 [64, 2, 4, 2], replicated, may hold values from 0 to 63, as said below
Outputs:
- query_grad: bfloat16 [4, 16384, 1024], P('tm', 'space')
- key_grad: bfloat16 [4, 16384, 1024], P('tm', 'space')
- value_grad: bfloat16 [4, 16384, 1024], P('tm', 'space')
- query_time_grad: bfloat16 [4, 16384, 1024], P('tm', 'space')
- key_time_grad: bfloat16 [4, 16384, 1024], P('tm', 'space')
Inputs may be any that keep to these rules, and one draw needn't show every extreme that they name: Every domain holds at least one block with fluid_mask 1. key_lists[s, b] holds first the 2 blocks of domain s in the order b, b + 1, ... modulo 2, then 1 distinct blocks of domain (s - 1) mod 64, then 1 distinct blocks of domain (s + 1) mod 64.
All inputs are finite; a program needn't handle non-finite values.
Results may differ from a plain program's by a relative error of at most 0.02.
Values may be sent and summed in bfloat16 or wider, within the bound.
No kernel may reach another device: no remote copies, remote signals or barrier semaphores. Data moves between devices by JAX's collectives and lax.ppermute only.
A program may use at most 128 MiB of HBM per device.

v0:
```python
import functools

import jax
import jax.numpy as jnp
from jax import lax
from jax.experimental import pallas as pl
from jax.experimental.pallas import tpu as pltpu
from jax.sharding import PartitionSpec as P

BLOCK = 128
H = 16
HD = 64
D = 1024
TOK = 256
QUARTER = 64
PAIRS = 8
SCALE = HD**-0.5
NEG = -1e30
F32 = jnp.float32
BF16 = jnp.bfloat16

VMEM_SPEC = pl.BlockSpec(memory_space=pltpu.VMEM)
SMEM_SPEC = pl.BlockSpec(memory_space=pltpu.SMEM)


def dot(a, b):
    return jnp.dot(a, b, preferred_element_type=F32)


def kernel_params(mib):
    return pltpu.CompilerParams(vmem_limit_bytes=mib * 1024 * 1024)


def cost(flops, nbytes):
    return pl.CostEstimate(flops=flops, bytes_accessed=nbytes, transcendentals=0)


def transposed(block):
    return block.astype(F32).T.astype(BF16)


def head_rows(block):
    row = lax.broadcasted_iota(jnp.int32, block.shape, 0)
    zero = jnp.zeros_like(block)
    return jnp.where(row < HD, block, zero), jnp.where(row < HD, zero, block)


def head_lanes(block):
    lane = lax.broadcasted_iota(jnp.int32, block.shape, 1)
    zero = jnp.zeros_like(block)
    return jnp.where(lane < HD, block, zero), jnp.where(lane < HD, zero, block)


def grouped_lanes(block_t):
    first, second = head_rows(block_t)
    return jnp.concatenate(
        [first[:, :BLOCK], second[:, :BLOCK], first[:, BLOCK:], second[:, BLOCK:]], axis=1
    )


def grouped_rows(block):
    first, second = head_lanes(block)
    return jnp.concatenate([first[:BLOCK], second[:BLOCK], first[BLOCK:], second[BLOCK:]], axis=0)


def stage_kernel(place, *refs):
    ins, outs = refs[:9], refs[9:]
    for d in range(3):
        for a in range(3):
            outs[d][a] = ins[d * 3 + a][...]


def stage(place, arrays):
    specs, operands = [], []
    for d in (1, 2, 3):
        for array in arrays:
            specs.append(
                pl.BlockSpec((QUARTER, D), functools.partial(lambda d, i, s: ((s[0] + d) % 4, 0), d))
            )
            operands.append(array)
    return pl.pallas_call(
        stage_kernel,
        grid_spec=pltpu.PrefetchScalarGridSpec(
            num_scalar_prefetch=1,
            grid=(1,),
            in_specs=specs,
            out_specs=[pl.BlockSpec((3, QUARTER, D), lambda i, s: (0, 0, 0))] * 3,
        ),
        out_shape=[jax.ShapeDtypeStruct((3, QUARTER, D), BF16)] * 3,
        compiler_params=kernel_params(24),
        cost_estimate=cost(0, 3 << 20),
        name="stage_time",
    )(place, *operands)


def listed(place, lists, side):
    return [lists[b * 4 + 2 + side] for b in range(2)]


def neighbour_rows(low_ref, high_ref, low_ids, high_ids, b, lanes):
    low = low_ref[pl.ds(pl.multiple_of(low_ids[b] * BLOCK, BLOCK), BLOCK), lanes]
    high = high_ref[pl.ds(pl.multiple_of(high_ids[b] * BLOCK, BLOCK), BLOCK), lanes]
    return jnp.concatenate([low, high], axis=0)


def forward_kernel(
    place, lists, fluid, occ, q, k, v, k_low, v_low, k_high, v_high,
    states, p1, p2, p3, probs, states_t, bias, scratch,
):
    me, dom = place[0], place[1]
    low_dom, high_dom = lax.rem(dom + 63, 64), lax.rem(dom + 1, 64)
    low_ids, high_ids = listed(place, lists, 0), listed(place, lists, 1)

    def column(row_id, keep):
        dead = occ[pl.ds(row_id, 1), :].astype(F32)
        row = jnp.where((dead > 0.5) | jnp.logical_not(keep), NEG, 0.0)
        return jnp.broadcast_to(row, (BLOCK, BLOCK)).T

    for b in range(2):
        keep = fluid[dom * 2 + b] > 0
        bias[b, 0:128] = column(dom * 2, keep)
        bias[b, 128:256] = column(dom * 2 + 1, keep)
        bias[b, 256:384] = column(low_dom * 2 + low_ids[b], keep)
        bias[b, 384:512] = column(high_dom * 2 + high_ids[b], keep)

    def pair(p):
        lanes = pl.ds(pl.multiple_of(p * 128, 128), 128)
        q_t = (q[:, lanes].astype(F32) * SCALE).T.astype(BF16)
        q_cols = grouped_lanes(q_t)
        v_t = transposed(v[:, lanes])
        s_own = dot(k[:, lanes], q_cols)
        outs = []
        for b in range(2):
            k_n = neighbour_rows(k_low, k_high, low_ids, high_ids, b, lanes)
            v_n_t = transposed(neighbour_rows(v_low, v_high, low_ids, high_ids, b, lanes))
            s_n = dot(k_n, q_cols[:, 256 * b : 256 * b + 256])
            bias_o, bias_n = bias[b, 0:256], bias[b, 256:512]
            halves = []
            for h in range(2):
                g = 2 * b + h
                so = s_own[:, g * 128 : g * 128 + 128] + bias_o
                sn = s_n[:, h * 128 : h * 128 + 128] + bias_n
                m = jnp.maximum(
                    jnp.max(jnp.maximum(so, sn), axis=0, keepdims=True), 0.0
                )
                eo, en = jnp.exp(so - m), jnp.exp(sn - m)
                total = jnp.exp(-m) + jnp.sum(eo + en, axis=0, keepdims=True)
                inv = 1.0 / total
                po, pn = (eo * inv).astype(BF16), (en * inv).astype(BF16)
                probs[p, 0:256, g * 128 : g * 128 + 128] = po
                probs[p, 256:512, g * 128 : g * 128 + 128] = pn
                halves.append(
                    dot(v_t[h * HD : h * HD + HD], po) + dot(v_n_t[h * HD : h * HD + HD], pn)
                )
            outs.append(jnp.concatenate(halves, axis=0))
        out_t = jnp.concatenate(outs, axis=1)
        states_t[pl.ds(pl.multiple_of(p * 128, 128), 128), :] = out_t.astype(BF16)
        scratch[:, lanes] = out_t.T.astype(BF16)

    pl.loop(0, PAIRS, unroll=2)(pair)
    states[...] = scratch[...]
    for d, piece in ((1, p1), (2, p2), (3, p3)):
        start = pl.multiple_of(lax.rem(me + d, 4) * QUARTER, QUARTER)
        piece[...] = scratch[pl.ds(start, QUARTER), :]


def window_forward(place, lists, fluid, occ, q, k, v, k_low, v_low, k_high, v_high):
    piece = jax.ShapeDtypeStruct((QUARTER, D), BF16)
    return pl.pallas_call(
        forward_kernel,
        in_specs=[SMEM_SPEC] * 3 + [VMEM_SPEC] * 8,
        out_specs=[VMEM_SPEC] * 6,
        out_shape=[
            jax.ShapeDtypeStruct((TOK, D), BF16), piece, piece, piece,
            jax.ShapeDtypeStruct((PAIRS, 512, 512), BF16),
            jax.ShapeDtypeStruct((D, TOK), BF16),
        ],
        scratch_shapes=[pltpu.VMEM((2, 512, BLOCK), F32), pltpu.VMEM((TOK, D), BF16)],
        compiler_params=kernel_params(32),
        cost_estimate=cost(4_000_000_000, 16 << 20),
        name="window_forward",
    )(place, lists, fluid, occ, q, k, v, k_low, v_low, k_high, v_high)


ROWS = 16
WIDE = 256


def head_sums():
    row = lax.broadcasted_iota(jnp.int32, (2 * WIDE, WIDE), 0) % WIDE
    lane = lax.broadcasted_iota(jnp.int32, (2 * WIDE, WIDE), 1)
    return jnp.where(row // HD == lane // HD, 1.0, 0.0).astype(BF16)


def pair_sums(left, right, ones):
    products = jnp.concatenate([a * b for a in left for b in right], axis=0)
    high = products.astype(BF16)
    low = (products - high.astype(F32)).astype(BF16)
    sums = dot(jnp.concatenate([high, low], axis=1), ones)
    return [[sums[(4 * t + u) * ROWS : (4 * t + u + 1) * ROWS] for u in range(4)] for t in range(4)]


def time_first_kernel(place, q0, k0, g0, m1, m2, m3, s0, s1, s2, s3, attn, ones_ref):
    ones_ref[...] = head_sums()
    outs = (s0, s1, s2, s3)

    def tile(i):
        rows = pl.ds(pl.multiple_of((i // 4) * ROWS, ROWS), ROWS)
        lanes = pl.ds(pl.multiple_of((i % 4) * WIDE, WIDE), WIDE)
        qs = [x.astype(F32) for x in (q0[rows, lanes], *(m[0, rows, lanes] for m in (m1, m2, m3)))]
        ks = [x.astype(F32) for x in (k0[rows, lanes], *(m[1, rows, lanes] for m in (m1, m2, m3)))]
        gs = [x.astype(F32) for x in (g0[rows, lanes], *(m[2, rows, lanes] for m in (m1, m2, m3)))]
        scores = pair_sums([x * SCALE for x in qs], ks, ones_ref[...])
        sums = list(gs)
        for t in range(4):
            row = scores[t]
            top = jnp.maximum(jnp.maximum(row[0], row[1]), jnp.maximum(row[2], row[3]))
            exps = [jnp.exp(x - top) for x in row]
            inv = 1.0 / ((exps[0] + exps[1]) + (exps[2] + exps[3]))
            for u in range(4):
                a = exps[u] * inv
                attn[4 * t + u, rows, lanes] = a.astype(BF16)
                sums[u] = sums[u] + a * gs[t]
        for u in range(4):
            outs[u][rows, lanes] = sums[u].astype(BF16)

    pl.loop(0, 16)(tile)


def quarter_spec():
    return pl.BlockSpec((QUARTER, D), lambda i, s: (s[0], 0))


def whole_spec(*shape):
    return pl.BlockSpec(shape, lambda i, s: (0,) * len(shape))


def time_first(place, q, k, g, m1, m2, m3):
    piece = jax.ShapeDtypeStruct((QUARTER, D), BF16)
    return pl.pallas_call(
        time_first_kernel,
        grid_spec=pltpu.PrefetchScalarGridSpec(
            num_scalar_prefetch=1,
            grid=(1,),
            in_specs=[quarter_spec()] * 3 + [whole_spec(3, QUARTER, D)] * 3,
            out_specs=[whole_spec(QUARTER, D)] * 4 + [whole_spec(16, QUARTER, D)],
            scratch_shapes=[pltpu.VMEM((2 * WIDE, WIDE), BF16)],
        ),
        out_shape=[piece] * 4 + [jax.ShapeDtypeStruct((16, QUARTER, D), BF16)],
        compiler_params=kernel_params(24),
        cost_estimate=cost(1_000_000_000, 8 << 20),
        name="time_first",
    )(place, q, k, g, m1, m2, m3)


def time_second_kernel(
    place, q0, k0, g0, m1, m2, m3, attn, x0, x1, x2, x3, o0, o1, o2, o3, ones_ref
):
    ones_ref[...] = head_sums()
    outs = (o0, o1, o2, o3)

    def tile(i):
        rows = pl.ds(pl.multiple_of((i // 4) * ROWS, ROWS), ROWS)
        lanes = pl.ds(pl.multiple_of((i % 4) * WIDE, WIDE), WIDE)
        gs = [x.astype(F32) for x in (g0[rows, lanes], *(m[2, rows, lanes] for m in (m1, m2, m3)))]
        xs = [x[rows, lanes].astype(F32) for x in (x0, x1, x2, x3)]
        dattn = pair_sums(gs, xs, ones_ref[...])
        qs = [x.astype(F32) for x in (q0[rows, lanes], *(m[0, rows, lanes] for m in (m1, m2, m3)))]
        ks = [x.astype(F32) for x in (k0[rows, lanes], *(m[1, rows, lanes] for m in (m1, m2, m3)))]
        key_sums = [None] * 4
        for t in range(4):
            a = [attn[4 * t + u, rows, lanes].astype(F32) for u in range(4)]
            mean = sum(x * y for x, y in zip(a[1:], dattn[t][1:], strict=True)) + a[0] * dattn[t][0]
            query_sum = None
            for u in range(4):
                grad = a[u] * (dattn[t][u] - mean)
                query_sum = grad * ks[u] if query_sum is None else query_sum + grad * ks[u]
                term = grad * qs[t]
                key_sums[u] = term if key_sums[u] is None else key_sums[u] + term
            outs[t][0, rows, lanes] = (query_sum * SCALE).astype(BF16)
        for u in range(4):
            outs[u][1, rows, lanes] = (key_sums[u] * SCALE).astype(BF16)

    pl.loop(0, 16)(tile)


def time_second(place, q, k, g, m1, m2, m3, attn, states, x1, x2, x3):
    piece = jax.ShapeDtypeStruct((2, QUARTER, D), BF16)
    return pl.pallas_call(
        time_second_kernel,
        grid_spec=pltpu.PrefetchScalarGridSpec(
            num_scalar_prefetch=1,
            grid=(1,),
            in_specs=[quarter_spec()] * 3
            + [whole_spec(3, QUARTER, D)] * 3
            + [whole_spec(16, QUARTER, D), quarter_spec()]
            + [whole_spec(QUARTER, D)] * 3,
            out_specs=[whole_spec(2, QUARTER, D)] * 4,
            scratch_shapes=[pltpu.VMEM((2 * WIDE, WIDE), BF16)],
        ),
        out_shape=[piece] * 4,
        compiler_params=kernel_params(24),
        cost_estimate=cost(1_000_000_000, 8 << 20),
        name="time_second",
    )(place, q, k, g, m1, m2, m3, attn, states, x1, x2, x3)


def grad_rows(sg, place, pieces):
    for d, piece in enumerate(pieces):
        start = pl.multiple_of(lax.rem(place[0] + d, 4) * QUARTER, QUARTER)
        sg[pl.ds(start, QUARTER), :] = piece[...]


def deltas(sg_t, st_t):
    product = sg_t.astype(F32) * st_t.astype(F32)
    first = jnp.sum(product[:HD], axis=0, keepdims=True)
    second = jnp.sum(product[HD:], axis=0, keepdims=True)
    return jnp.concatenate(
        [first[:, :BLOCK], second[:, :BLOCK], first[:, BLOCK:], second[:, BLOCK:]], axis=1
    )


def back_sides_kernel(
    place, lists, q, k_low, v_low, k_high, v_high, probs, states_t, g0, g1, g2, g3,
    to_low, to_high, query_part, sg,
):
    low_ids, high_ids = listed(place, lists, 0), listed(place, lists, 1)
    grad_rows(sg, place, (g0, g1, g2, g3))

    def pair(p):
        lanes = pl.ds(pl.multiple_of(p * 128, 128), 128)
        rows = pl.ds(pl.multiple_of(p * 128, 128), 128)
        sg_p = sg[:, lanes]
        sg_t = transposed(sg_p)
        sg_cols, sg_rows, q_rows = grouped_lanes(sg_t), grouped_rows(sg_p), grouped_rows(q[:, lanes])
        delta = deltas(sg_t, states_t[rows, :])
        key_parts, value_parts = [], []
        for b in range(2):
            cols = slice(256 * b, 256 * b + 256)
            k_n = neighbour_rows(k_low, k_high, low_ids, high_ids, b, lanes)
            v_n = neighbour_rows(v_low, v_high, low_ids, high_ids, b, lanes)
            k_n_t = transposed(k_n)
            dp = dot(v_n, sg_cols[:, cols])
            pr = probs[p, 256:512, cols]
            ds = (pr.astype(F32) * (dp - delta[:, cols])).astype(BF16)
            query_part[rows, b * 128 : b * 128 + 128] = jnp.concatenate(
                [dot(k_n_t[:HD], ds[:, :BLOCK]), dot(k_n_t[HD:], ds[:, BLOCK:])], axis=0
            )
            key_parts.append(dot(ds, q_rows[cols]) * SCALE)
            value_parts.append(dot(pr, sg_rows[cols]))
        for n, parts in enumerate((key_parts, value_parts)):
            for ids, out, side in ((low_ids, to_low, 0), (high_ids, to_high, 1)):
                for j in range(2):
                    total = sum(
                        jnp.where(ids[b] == j, parts[b][side * 128 : side * 128 + 128], 0.0)
                        for b in range(2)
                    )
                    out[n, j * 128 : j * 128 + 128, lanes] = total.astype(BF16)

    pl.loop(0, PAIRS, unroll=2)(pair)


def back_sides(place, lists, q, k_low, v_low, k_high, v_high, probs, states_t, pieces):
    message = jax.ShapeDtypeStruct((2, TOK, D), BF16)
    return pl.pallas_call(
        back_sides_kernel,
        in_specs=[SMEM_SPEC] * 2 + [VMEM_SPEC] * 11,
        out_specs=[VMEM_SPEC] * 3,
        out_shape=[message, message, jax.ShapeDtypeStruct((D, TOK), F32)],
        scratch_shapes=[pltpu.VMEM((TOK, D), BF16)],
        compiler_params=kernel_params(32),
        cost_estimate=cost(6_000_000_000, 16 << 20),
        name="back_sides",
    )(place, lists, q, k_low, v_low, k_high, v_high, probs, states_t, *pieces)


def back_own_kernel(
    place, q, k, v, probs, states_t, query_part, g0, g1, g2, g3, query_grad, totals, sg
):
    grad_rows(sg, place, (g0, g1, g2, g3))

    def pair(p):
        lanes = pl.ds(pl.multiple_of(p * 128, 128), 128)
        rows = pl.ds(pl.multiple_of(p * 128, 128), 128)
        sg_p = sg[:, lanes]
        sg_t = transposed(sg_p)
        sg_cols, sg_rows, q_rows = grouped_lanes(sg_t), grouped_rows(sg_p), grouped_rows(q[:, lanes])
        delta = deltas(sg_t, states_t[rows, :])
        k_t = transposed(k[:, lanes])
        dp = dot(v[:, lanes], sg_cols)
        pr = probs[p, 0:256, :]
        ds = (pr.astype(F32) * (dp - delta)).astype(BF16)
        cols = [
            jnp.concatenate(
                [
                    dot(k_t[:HD], ds[:, 256 * b : 256 * b + 128]),
                    dot(k_t[HD:], ds[:, 256 * b + 128 : 256 * b + 256]),
                ],
                axis=0,
            )
            for b in range(2)
        ]
        query_t = jnp.concatenate(cols, axis=1) + query_part[rows, :]
        query_grad[:, lanes] = (query_t * SCALE).T.astype(BF16)
        totals[0, :, lanes] = dot(ds, q_rows) * SCALE
        totals[1, :, lanes] = dot(pr, sg_rows)

    pl.loop(0, PAIRS, unroll=2)(pair)


def back_own(place, q, k, v, probs, states_t, query_part, pieces):
    return pl.pallas_call(
        back_own_kernel,
        in_specs=[SMEM_SPEC] + [VMEM_SPEC] * 10,
        out_specs=[VMEM_SPEC] * 2,
        out_shape=[
            jax.ShapeDtypeStruct((TOK, D), BF16),
            jax.ShapeDtypeStruct((2, TOK, D), F32),
        ],
        scratch_shapes=[pltpu.VMEM((TOK, D), BF16)],
        compiler_params=kernel_params(32),
        cost_estimate=cost(6_000_000_000, 16 << 20),
        name="back_own",
    )(place, q, k, v, probs, states_t, query_part, *pieces)


def finish_kernel(place, totals, low, high, t0, t1, t2, t3, key_grad, value_grad, query_t, key_t):
    for n, out in ((0, key_grad), (1, value_grad)):
        out[...] = (totals[n] + low[n].astype(F32) + high[n].astype(F32)).astype(BF16)
    for d, piece in enumerate((t0, t1, t2, t3)):
        start = pl.multiple_of(lax.rem(place[0] + d, 4) * QUARTER, QUARTER)
        query_t[pl.ds(start, QUARTER), :] = piece[0]
        key_t[pl.ds(start, QUARTER), :] = piece[1]


def finish(place, totals, low, high, pieces):
    return pl.pallas_call(
        finish_kernel,
        in_specs=[SMEM_SPEC] + [VMEM_SPEC] * 7,
        out_specs=[VMEM_SPEC] * 4,
        out_shape=[jax.ShapeDtypeStruct((TOK, D), BF16)] * 4,
        compiler_params=kernel_params(24),
        cost_estimate=cost(0, 8 << 20),
        name="finish",
    )(place, totals, low, high, *pieces)


def body(
    queries, key_vectors, value_vectors, query_time, key_time, out_grad, fluid_mask, occupancy, key_lists
):
    q, k, v = queries[0], key_vectors[0], value_vectors[0]
    qt, kt, og = query_time[0], key_time[0], out_grad[0]
    me, dom = lax.axis_index("tm"), lax.axis_index("space")
    place = jnp.stack([me, dom]).astype(jnp.int32)
    lists = lax.dynamic_index_in_dim(key_lists, dom, 0, keepdims=False)[:, :, 1].reshape(-1)
    occ = occupancy.reshape(-1, BLOCK)

    domains, steps = lax.axis_size("space"), lax.axis_size("tm")
    up = [(i, (i + 1) % domains) for i in range(domains)]
    down = [(i, (i - 1) % domains) for i in range(domains)]

    def shift(x, d):
        return lax.ppermute(x, "tm", [(i, (i + d) % steps) for i in range(steps)])

    sent = stage(place, (qt, kt, og))
    arrived = {(4 - d) % 4: shift(sent[d - 1], d) for d in (1, 3, 2)}
    ms = (arrived[1], arrived[2], arrived[3])
    k_low, v_low = lax.ppermute(k, "space", up), lax.ppermute(v, "space", up)
    k_high, v_high = lax.ppermute(k, "space", down), lax.ppermute(v, "space", down)

    states, p1, p2, p3, probs, states_t = window_forward(
        place, lists, fluid_mask, occ, q, k, v, k_low, v_low, k_high, v_high
    )
    *grads, attn = time_first(place, qt, kt, og, *ms)
    home = {(4 - d) % 4: shift(grads[d], d) for d in (1, 3, 2)}
    grad_pieces = (grads[0], home[1], home[2], home[3])

    pieces = (None, p1, p2, p3)
    there = {(4 - d) % 4: shift(pieces[d], d) for d in (1, 3, 2)}
    back = time_second(place, qt, kt, og, *ms, attn, states, there[1], there[2], there[3])
    returned = {(4 - d) % 4: shift(back[d], d) for d in (1, 3, 2)}

    to_low, to_high, query_part = back_sides(
        place, lists, q, k_low, v_low, k_high, v_high, probs, states_t, grad_pieces
    )
    from_high = lax.ppermute(to_low, "space", down)
    from_low = lax.ppermute(to_high, "space", up)
    query_grad, totals = back_own(place, q, k, v, probs, states_t, query_part, grad_pieces)
    key_grad, value_grad, query_time_grad, key_time_grad = finish(
        place, totals, from_low, from_high, (back[0], returned[1], returned[2], returned[3])
    )
    return tuple(
        x[None] for x in (query_grad, key_grad, value_grad, query_time_grad, key_time_grad)
    )


def solution(mesh):
    split = P("tm", "space", None)
    return jax.shard_map(
        body,
        mesh=mesh,
        in_specs=(split,) * 6 + (P(),) * 3,
        out_specs=(split,) * 5,
        check_vma=False,
    )
```

profile of v0, /device:TPU:103, one launch (start us, length us, event | category | flops | bytes accessed | tf_op | source)
XLA Modules:
  0.0 100.3 jit_solution(4800105384829091516)
XLA Ops:
  0.6 0.0 copy-start
  0.7 0.1 pad_add_fusion.place
  0.7 0.0 copy-start.1
  0.7 1.0 %copy-done.1 = bf16[1,256,1024]{2,1,0:T(8,128)(2,1)S(1)} copy-done((bf16[1,256,1024]{2,1,0:T(8,128)(2,1)S(1)}, bf16[1,256,1024]{2,1,0:T(8,128)(2,1)}, u32[]{:S(2)}) %copy-start.1) | copy-done | bytes 524312
  1.8 0.0 copy-start.3
  1.8 1.0 %copy-done.3 = bf16[1,256,1024]{2,1,0:T(8,128)(2,1)S(1)} copy-done((bf16[1,256,1024]{2,1,0:T(8,128)(2,1)S(1)}, bf16[1,256,1024]{2,1,0:T(8,128)(2,1)}, u32[]{:S(2)}) %copy-start.3) | copy-done | bytes 524312
  2.8 1.0 %copy-done.5 = bf16[1,256,1024]{2,1,0:T(8,128)(2,1)S(1)} copy-done((bf16[1,256,1024]{2,1,0:T(8,128)(2,1)S(1)}, bf16[1,256,1024]{2,1,0:T(8,128)(2,1)}, u32[]{:S(2)}) %copy-start.5) | copy-done | bytes 524312
  3.9 0.0 copy-start.2
  3.9 0.0 copy-start.4
  3.9 0.0 copy-start.6
  3.9 1.4 %stage_time.1 = (bf16[3,64,1024]{2,1,0:T(8,128)(2,1)}, bf16[3,64,1024]{2,1,0:T(8,128)(2,1)S(1)}, bf16[3,64,1024]{2,1,0:T(8,128)(2,1)S(1)}) custom-call(s32[2]{0:T(128)S(1)} %pad_add_fusion.place, bf16[256,1024]{1,0:T(8,128)(2,1)S(1)} %bitcast.15, bf16[256,1024]{1,0:T(8,128)(2,1)S(1)} %bitcast.20, bf16[256,1024]{1,0:T(8,128)(2,1)S(1)} %bitcast.25, ...), custom_call_target="tpu_custom_call" | custom-call | bytes 3145728 | tf_op jit(solution)/shard_map/stage_time/pallas_call | solution.py:81
  5.2 0.0 copy-start.7
  5.2 2.7 %collective-permute-start.4 = (bf16[3,64,1024]{2,1,0:T(8,128)(2,1)S(1)}, bf16[3,64,1024]{2,1,0:T(8,128)(2,1)S(1)}, u32[]{:S(2)}, u32[]{:S(2)}) collective-permute-start(bf16[3,64,1024]{2,1,0:T(8,128)(2,1)S(1)} %get-tuple-element.34), channel_id=1, source_target_pairs={{0,3},{1,0},{2,1},{3,2},{4,7},{5,4},{6,5},{7,6},{8,11},{9,8},{10,9... | collective-permute-start | bytes 1179656 | tf_op jit(solution)/shard_map/ppermute | solution.py:463
  8.0 0.3 collective-permute-start.5
  8.3 1.2 %collective-permute-start.2 = (bf16[256,1024]{1,0:T(8,128)(2,1)}, bf16[256,1024]{1,0:T(8,128)(2,1)}, u32[]{:S(2)}, u32[]{:S(2)}) collective-permute-start(bf16[256,1024]{1,0:T(8,128)(2,1)} %bitcast.3.k), channel_id=1, source_target_pairs={{0,252},{4,0},{8,4},{12,8},{16,12},{20,16},{24,20},{28,24},{32,28}... | collective-permute-start | bytes 1572872 | tf_op jit(solution)/shard_map/ppermute | solution.py:469
  9.6 2.7 %collective-permute-start = (bf16[256,1024]{1,0:T(8,128)(2,1)}, bf16[256,1024]{1,0:T(8,128)(2,1)}, u32[]{:S(2)}, u32[]{:S(2)}) collective-permute-start(bf16[256,1024]{1,0:T(8,128)(2,1)} %bitcast.3.k), channel_id=1, source_target_pairs={{0,4},{4,8},{8,12},{12,16},{16,20},{20,24},{24,28},{28,32},{32,36}... | collective-permute-start | bytes 1572872 | tf_op jit(solution)/shard_map/ppermute | solution.py:468
  12.3 0.0 collective-permute-start.3
  12.3 4.5 %collective-permute-done.4.m1 = bf16[3,64,1024]{2,1,0:T(8,128)(2,1)S(1)} collective-permute-done((bf16[3,64,1024]{2,1,0:T(8,128)(2,1)S(1)}, bf16[3,64,1024]{2,1,0:T(8,128)(2,1)S(1)}, u32[]{:S(2)}, u32[]{:S(2)}) %collective-permute-start.4) | collective-permute-done | bytes 393248 | tf_op jit(solution)/shard_map/ppermute | solution.py:463
  16.8 11.7 %collective-permute-start.1 = (bf16[256,1024]{1,0:T(8,128)(2,1)}, bf16[256,1024]{1,0:T(8,128)(2,1)}, u32[]{:S(2)}, u32[]{:S(2)}) collective-permute-start(bf16[256,1024]{1,0:T(8,128)(2,1)} %bitcast.4.v), channel_id=1, source_target_pairs={{0,4},{4,8},{8,12},{12,16},{16,20},{20,24},{24,28},{28,32},{32,36}... | collective-permute-start | bytes 1572872 | tf_op jit(solution)/shard_map/ppermute | solution.py:468
  28.5 0.0 collective-permute-done.5.m2
  28.5 0.0 collective-permute-start.6
  28.5 0.0 copy-done
  28.5 0.1 constant_dynamic-slice_fusion
  28.6 0.1 copy.14
  28.7 0.1 reshape_squeeze.3.lists
  28.8 10.1 %collective-permute-done.6.m3 = bf16[3,64,1024]{2,1,0:T(8,128)(2,1)S(1)} collective-permute-done((bf16[3,64,1024]{2,1,0:T(8,128)(2,1)}, bf16[3,64,1024]{2,1,0:T(8,128)(2,1)S(1)}, u32[]{:S(2)}, u32[]{:S(2)}) %collective-permute-start.6) | collective-permute-done | bytes 393248 | tf_op jit(solution)/shard_map/ppermute | solution.py:463
  38.9 0.0 copy-done.2
  38.9 0.0 copy-done.4
  38.9 0.0 copy-done.6
  38.9 5.0 %time_first.1 = (bf16[64,1024]{1,0:T(8,128)(2,1)S(1)}, bf16[64,1024]{1,0:T(8,128)(2,1)S(1)}, bf16[64,1024]{1,0:T(8,128)(2,1)S(1)}, bf16[64,1024]{1,0:T(8,128)(2,1)S(1)}, bf16[16,64,1024]{2,1,0:T(8,128)(2,1)S(1)}) custom-call(s32[2]{0:T(128)S(1)} %pad_add_fusion.place, bf16[256,1024]{1,0:T(8,128)(2,1)S(1)} %bitcast.18, bf16[256,1024]{1,0:T(8,128)(2,1)S(1)} %bitcast.23, ...), custom_call_target="tpu_custom_call" | custom-call | flops 1000000000 | bytes 8388608 | tf_op jit(solution)/shard_map/time_first/pallas_call | solution.py:240
  43.9 1.8 %collective-permute-start.7 = (bf16[64,1024]{1,0:T(8,128)(2,1)S(1)}, bf16[64,1024]{1,0:T(8,128)(2,1)S(1)}, u32[]{:S(2)}, u32[]{:S(2)}) collective-permute-start(bf16[64,1024]{1,0:T(8,128)(2,1)S(1)} %get-tuple-element.38), channel_id=1, source_target_pairs={{0,3},{1,0},{2,1},{3,2},{4,7},{5,4},{6,5},{7,6},{8,11},{9,8},{10,9... | collective-permute-start | bytes 393224 | tf_op jit(solution)/shard_map/ppermute | solution.py:463
  45.8 0.0 collective-permute-done.2.k_high
  45.8 0.1 collective-permute-start.8
  45.9 0.0 collective-permute-done.k_low
  45.9 0.5 collective-permute-start.9
  46.5 0.0 collective-permute-done.3.v_high
  46.5 0.0 collective-permute-done.1.v_low
  46.5 0.0 copy-done.7
  46.5 0.0 copy-done.8
  46.5 0.0 copy-done.9
  46.5 8.2 %window_forward.1 = (bf16[256,1024]{1,0:T(8,128)(2,1)S(1)}, bf16[64,1024]{1,0:T(8,128)(2,1)S(1)}, bf16[64,1024]{1,0:T(8,128)(2,1)S(1)}, bf16[64,1024]{1,0:T(8,12...) custom-call(s32[2]{0:T(128)S(1)} %pad_add_fusion.place, s32[8]{0:T(128)S(1)} %reshape_squeeze.3.lists, ...), custom_call_target="tpu_custom_call" | custom-call | flops 4000000000 | bytes 16777216 | tf_op jit(solution)/shard_map/window_forward/pallas_call | solution.py:169
  54.7 0.0 collective-permute-done.7.g1
  54.7 0.0 collective-permute-done.8.g2
  54.7 0.0 collective-permute-done.9.g3
  54.7 7.2 %back_sides.1 = (bf16[2,256,1024]{2,1,0:T(8,128)(2,1)S(1)}, bf16[2,256,1024]{2,1,0:T(8,128)(2,1)S(1)}, f32[1024,256]{1,0:T(8,128)S(1)}) custom-call(s32[2]{0:T(128)S(1)} %pad_add_fusion.place, s32[8]{0:T(128)S(1)} %reshape_squeeze.3.lists, bf16[256,1024]{1,0:T(8,128)(2,1)S(1)} %bitcast.31, bf16[256,1024]{1,0:T(8,128)(2,1)} %collective-permute-done.k_low, ...), custom_call_target="tpu_custom_call" | custom-call | flops 6000000000 | bytes 16777216 | tf_op jit(solution)/shard_map/back_sides/pallas_call | solution.py:365
  61.9 4.0 %collective-permute-start.10 = (bf16[2,256,1024]{2,1,0:T(8,128)(2,1)S(1)}, bf16[2,256,1024]{2,1,0:T(8,128)(2,1)S(1)}, u32[]{:S(2)}, u32[]{:S(2)}) collective-permute-start(bf16[2,256,1024]{2,1,0:T(8,128)(2,1)S(1)} %get-tuple-element.44), channel_id=1, source_target_pairs={{0,4},{4,8},{8,12},{12,16},{16,20},{20,24},{24,28},{28,32},{32,36}... | collective-permute-start | bytes 3145736 | tf_op jit(solution)/shard_map/ppermute | solution.py:487
  65.9 0.0 collective-permute-start.11
  65.9 1.9 %collective-permute-start.12 = (bf16[64,1024]{1,0:T(8,128)(2,1)S(1)}, bf16[64,1024]{1,0:T(8,128)(2,1)S(1)}, u32[]{:S(2)}, u32[]{:S(2)}) collective-permute-start(bf16[64,1024]{1,0:T(8,128)(2,1)S(1)} %get-tuple-element.48), channel_id=1, source_target_pairs={{0,3},{1,0},{2,1},{3,2},{4,7},{5,4},{6,5},{7,6},{8,11},{9,8},{10,9... | collective-permute-start | bytes 393224 | tf_op jit(solution)/shard_map/ppermute | solution.py:463
  67.8 2.0 %collective-permute-start.13 = (bf16[64,1024]{1,0:T(8,128)(2,1)S(1)}, bf16[64,1024]{1,0:T(8,128)(2,1)S(1)}, u32[]{:S(2)}, u32[]{:S(2)}) collective-permute-start(bf16[64,1024]{1,0:T(8,128)(2,1)S(1)} %get-tuple-element.49), channel_id=1, source_target_pairs={{0,2},{1,3},{2,0},{3,1},{4,6},{5,7},{6,4},{7,5},{8,10},{9,11},{10,... | collective-permute-start | bytes 393224 | tf_op jit(solution)/shard_map/ppermute | solution.py:463
  69.8 0.0 collective-permute-start.14
  69.8 3.7 %collective-permute-done.12.x1 = bf16[64,1024]{1,0:T(8,128)(2,1)S(1)} collective-permute-done((bf16[64,1024]{1,0:T(8,128)(2,1)S(1)}, bf16[64,1024]{1,0:T(8,128)(2,1)S(1)}, u32[]{:S(2)}, u32[]{:S(2)}) %collective-permute-start.12) | collective-permute-done | bytes 131104 | tf_op jit(solution)/shard_map/ppermute | solution.py:463
  73.5 1.1 %collective-permute-done.13.x2 = bf16[64,1024]{1,0:T(8,128)(2,1)S(1)} collective-permute-done((bf16[64,1024]{1,0:T(8,128)(2,1)S(1)}, bf16[64,1024]{1,0:T(8,128)(2,1)S(1)}, u32[]{:S(2)}, u32[]{:S(2)}) %collective-permute-start.13) | collective-permute-done | bytes 131104 | tf_op jit(solution)/shard_map/ppermute | solution.py:463
  74.6 2.3 %collective-permute-done.14.x3 = bf16[64,1024]{1,0:T(8,128)(2,1)S(1)} collective-permute-done((bf16[64,1024]{1,0:T(8,128)(2,1)S(1)}, bf16[64,1024]{1,0:T(8,128)(2,1)S(1)}, u32[]{:S(2)}, u32[]{:S(2)}) %collective-permute-start.14) | collective-permute-done | bytes 131104 | tf_op jit(solution)/shard_map/ppermute | solution.py:463
  76.9 5.0 %time_second.1 = (bf16[2,64,1024]{2,1,0:T(8,128)(2,1)S(1)}, bf16[2,64,1024]{2,1,0:T(8,128)(2,1)S(1)}, bf16[2,64,1024]{2,1,0:T(8,128)(2,1)S(1)}, bf16[2,64,1024]{2,1,0:T(8,128)(2,1)S(1)}) custom-call(s32[2]{0:T(128)S(1)} %pad_add_fusion.place, bf16[256,1024]{1,0:T(8,128)(2,1)S(1)} %bitcast.19, bf16[256,1024]{1,0:T(8,128)(2,1)S(1)} %bitcast.24, ...), custom_call_target="tpu_custom_call" | custom-call | flops 1000000000 | bytes 8388608 | tf_op jit(solution)/shard_map/time_second/pallas_call | solution.py:289
  81.9 1.0 collective-permute-start.15
  82.9 0.0 collective-permute-start.16
  82.9 0.7 collective-permute-start.17
  83.6 6.0 %back_own.1 = (bf16[256,1024]{1,0:T(8,128)(2,1)}, f32[2,256,1024]{2,1,0:T(8,128)S(1)}) custom-call(s32[2]{0:T(128)S(1)} %pad_add_fusion.place, bf16[256,1024]{1,0:T(8,128)(2,1)S(1)} %bitcast.32, bf16[256,1024]{1,0:T(8,128)(2,1)} %bitcast.3.k, bf16[256,1024]{1,0:T(8,128)(2,1)} %bitcast.4.v, bf16[8,512,512]{2,1,0:T(8,128)(2,1)S(1)} %get-tuple-element.32.probs, ...), custom_call_target="tpu_custom_call" | custom-call | flops 6000000000 | bytes 16777216 | tf_op jit(solution)/shard_map/back_own/pallas_call | solution.py:412
  89.6 0.1 collective-permute-done.15.t1
  89.6 2.2 %collective-permute-done.16.t2 = bf16[2,64,1024]{2,1,0:T(8,128)(2,1)S(1)} collective-permute-done((bf16[2,64,1024]{2,1,0:T(8,128)(2,1)S(1)}, bf16[2,64,1024]{2,1,0:T(8,128)(2,1)S(1)}, u32[]{:S(2)}, u32[]{:S(2)}) %collective-permute-start.16) | collective-permute-done | bytes 262176 | tf_op jit(solution)/shard_map/ppermute | solution.py:463
  91.8 6.4 %collective-permute-done.17.t3 = bf16[2,64,1024]{2,1,0:T(8,128)(2,1)S(1)} collective-permute-done((bf16[2,64,1024]{2,1,0:T(8,128)(2,1)S(1)}, bf16[2,64,1024]{2,1,0:T(8,128)(2,1)S(1)}, u32[]{:S(2)}, u32[]{:S(2)}) %collective-permute-start.17) | collective-permute-done | bytes 262176 | tf_op jit(solution)/shard_map/ppermute | solution.py:463
  98.2 0.0 collective-permute-done.10.low
  98.2 0.0 collective-permute-done.11.high
  98.2 2.1 %finish.1 = (bf16[256,1024]{1,0:T(8,128)(2,1)}, bf16[256,1024]{1,0:T(8,128)(2,1)}, bf16[256,1024]{1,0:T(8,128)(2,1)}, bf16[256,1024]{1,0:T(8,128)(2,1)}) custom-call(s32[2]{0:T(128)S(1)} %pad_add_fusion.place, f32[2,256,1024]{2,1,0:T(8,128)S(1)} %get-tuple-element.43.totals, bf16[2,256,1024]{2,1,0:T(8,128)(2,1)S(1)} %collective-permute-done.10.low, ...), custom_call_target="tpu_custom_call" | custom-call | bytes 8388608 | tf_op jit(solution)/shard_map/finish/pallas_call | solution.py:437
  (4 shorter events, 0.0 us)
Async XLA Ops:
  0.6 27.8 %copy-start = (s32[64,2,4,2]{0,3,2,1:T(2,128)S(1)}, s32[64,2,4,2]{0,3,2,1:T(2,128)}, u32[]{:S(2)}) copy-start(s32[64,2,4,2]{0,3,2,1:T(2,128)} %param.17) | copy-start | bytes 12292
  0.7 1.0 %copy-start.1 = (bf16[1,256,1024]{2,1,0:T(8,128)(2,1)S(1)}, bf16[1,256,1024]{2,1,0:T(8,128)(2,1)}, u32[]{:S(2)}) copy-start(bf16[1,256,1024]{2,1,0:T(8,128)(2,1)} %param.12) | copy-start | bytes 1572868
  1.8 1.0 %copy-start.3 = (bf16[1,256,1024]{2,1,0:T(8,128)(2,1)S(1)}, bf16[1,256,1024]{2,1,0:T(8,128)(2,1)}, u32[]{:S(2)}) copy-start(bf16[1,256,1024]{2,1,0:T(8,128)(2,1)} %param.13) | copy-start | bytes 1572868
  2.8 1.0 %copy-start.5 = (bf16[1,256,1024]{2,1,0:T(8,128)(2,1)S(1)}, bf16[1,256,1024]{2,1,0:T(8,128)(2,1)}, u32[]{:S(2)}) copy-start(bf16[1,256,1024]{2,1,0:T(8,128)(2,1)} %param.14) | copy-start | bytes 1572868
  3.9 35.1 %copy-start.2 = (bf16[1,256,1024]{2,1,0:T(8,128)(2,1)S(1)}, bf16[1,256,1024]{2,1,0:T(8,128)(2,1)}, u32[]{:S(2)}) copy-start(bf16[1,256,1024]{2,1,0:T(8,128)(2,1)} %param.12) | copy-start | bytes 1572868
  3.9 35.1 %copy-start.4 = (bf16[1,256,1024]{2,1,0:T(8,128)(2,1)S(1)}, bf16[1,256,1024]{2,1,0:T(8,128)(2,1)}, u32[]{:S(2)}) copy-start(bf16[1,256,1024]{2,1,0:T(8,128)(2,1)} %param.13) | copy-start | bytes 1572868
  3.9 35.1 %copy-start.6 = (bf16[1,256,1024]{2,1,0:T(8,128)(2,1)S(1)}, bf16[1,256,1024]{2,1,0:T(8,128)(2,1)}, u32[]{:S(2)}) copy-start(bf16[1,256,1024]{2,1,0:T(8,128)(2,1)} %param.14) | copy-start | bytes 1572868
  5.2 41.2 %copy-start.7 = (bf16[1,256,1024]{2,1,0:T(8,128)(2,1)S(1)}, bf16[1,256,1024]{2,1,0:T(8,128)(2,1)}, u32[]{:S(2)}) copy-start(bf16[1,256,1024]{2,1,0:T(8,128)(2,1)} %param.9) | copy-start | bytes 1572868
  5.2 41.2 %copy-start.8 = (s32[16384]{0:T(1024)S(1)}, s32[16384]{0:T(1024)}, u32[]{:S(2)}) copy-start(s32[16384]{0:T(1024)} %param.16) | copy-start | bytes 196612
  5.2 41.2 %copy-start.9 = (s32[128]{0:T(128)S(1)}, s32[128]{0:T(128)}, u32[]{:S(2)}) copy-start(s32[128]{0:T(128)} %fluid.1) | copy-start | bytes 1540
  5.2 11.5 %collective-permute-start.4 = (bf16[3,64,1024]{2,1,0:T(8,128)(2,1)S(1)}, bf16[3,64,1024]{2,1,0:T(8,128)(2,1)S(1)}, u32[]{:S(2)}, u32[]{:S(2)}) collective-permute-start(bf16[3,64,1024]{2,1,0:T(8,128)(2,1)S(1)} %get-tuple-element.34), channel_id=1, source_target_pairs={{0,3},{1,0},{2,1},{3,2},{4,7},{5,4},{6,5},{7,6},{8,11},{9,8},{10,9... | collective-permute-start | bytes 1179656 | tf_op jit(solution)/shard_map/ppermute | solution.py:463
  8.0 20.5 %collective-permute-start.5 = (bf16[3,64,1024]{2,1,0:T(8,128)(2,1)S(1)}, bf16[3,64,1024]{2,1,0:T(8,128)(2,1)S(1)}, u32[]{:S(2)}, u32[]{:S(2)}) collective-permute-start(bf16[3,64,1024]{2,1,0:T(8,128)(2,1)S(1)} %get-tuple-element.35), channel_id=1, source_target_pairs={{0,2},{1,3},{2,0},{3,1},{4,6},{5,7},{6,4},{7,5},{8,10},{9,11},{10,... | collective-permute-start | bytes 1179656 | tf_op jit(solution)/shard_map/ppermute | solution.py:463
  8.3 37.4 %collective-permute-start.2 = (bf16[256,1024]{1,0:T(8,128)(2,1)}, bf16[256,1024]{1,0:T(8,128)(2,1)}, u32[]{:S(2)}, u32[]{:S(2)}) collective-permute-start(bf16[256,1024]{1,0:T(8,128)(2,1)} %bitcast.3.k), channel_id=1, source_target_pairs={{0,252},{4,0},{8,4},{12,8},{16,12},{20,16},{24,20},{28,24},{32,28}... | collective-permute-start | bytes 1572872 | tf_op jit(solution)/shard_map/ppermute | solution.py:469
  9.6 36.4 %collective-permute-start = (bf16[256,1024]{1,0:T(8,128)(2,1)}, bf16[256,1024]{1,0:T(8,128)(2,1)}, u32[]{:S(2)}, u32[]{:S(2)}) collective-permute-start(bf16[256,1024]{1,0:T(8,128)(2,1)} %bitcast.3.k), channel_id=1, source_target_pairs={{0,4},{4,8},{8,12},{12,16},{16,20},{20,24},{24,28},{28,32},{32,36}... | collective-permute-start | bytes 1572872 | tf_op jit(solution)/shard_map/ppermute | solution.py:468
  12.3 34.2 %collective-permute-start.3 = (bf16[256,1024]{1,0:T(8,128)(2,1)}, bf16[256,1024]{1,0:T(8,128)(2,1)}, u32[]{:S(2)}, u32[]{:S(2)}) collective-permute-start(bf16[256,1024]{1,0:T(8,128)(2,1)} %bitcast.4.v), channel_id=1, source_target_pairs={{0,252},{4,0},{8,4},{12,8},{16,12},{20,16},{24,20},{28,24},{32,28}... | collective-permute-start | bytes 1572872 | tf_op jit(solution)/shard_map/ppermute | solution.py:469
  16.8 29.7 %collective-permute-start.1 = (bf16[256,1024]{1,0:T(8,128)(2,1)}, bf16[256,1024]{1,0:T(8,128)(2,1)}, u32[]{:S(2)}, u32[]{:S(2)}) collective-permute-start(bf16[256,1024]{1,0:T(8,128)(2,1)} %bitcast.4.v), channel_id=1, source_target_pairs={{0,4},{4,8},{8,12},{12,16},{16,20},{20,24},{24,28},{28,32},{32,36}... | collective-permute-start | bytes 1572872 | tf_op jit(solution)/shard_map/ppermute | solution.py:468
  28.5 10.5 %collective-permute-start.6 = (bf16[3,64,1024]{2,1,0:T(8,128)(2,1)}, bf16[3,64,1024]{2,1,0:T(8,128)(2,1)S(1)}, u32[]{:S(2)}, u32[]{:S(2)}) collective-permute-start(bf16[3,64,1024]{2,1,0:T(8,128)(2,1)} %get-tuple-element.36), channel_id=1, source_target_pairs={{0,1},{1,2},{2,3},{3,0},{4,5},{5,6},{6,7},{7,4},{8,9},{9,10},{10,1... | collective-permute-start | bytes 1179656 | tf_op jit(solution)/shard_map/ppermute | solution.py:463
  43.9 10.7 %collective-permute-start.7 = (bf16[64,1024]{1,0:T(8,128)(2,1)S(1)}, bf16[64,1024]{1,0:T(8,128)(2,1)S(1)}, u32[]{:S(2)}, u32[]{:S(2)}) collective-permute-start(bf16[64,1024]{1,0:T(8,128)(2,1)S(1)} %get-tuple-element.38), channel_id=1, source_target_pairs={{0,3},{1,0},{2,1},{3,2},{4,7},{5,4},{6,5},{7,6},{8,11},{9,8},{10,9... | collective-permute-start | bytes 393224 | tf_op jit(solution)/shard_map/ppermute | solution.py:463
  45.8 8.9 %collective-permute-start.8 = (bf16[64,1024]{1,0:T(8,128)(2,1)S(1)}, bf16[64,1024]{1,0:T(8,128)(2,1)S(1)}, u32[]{:S(2)}, u32[]{:S(2)}) collective-permute-start(bf16[64,1024]{1,0:T(8,128)(2,1)S(1)} %get-tuple-element.39), channel_id=1, source_target_pairs={{0,2},{1,3},{2,0},{3,1},{4,6},{5,7},{6,4},{7,5},{8,10},{9,11},{10,... | collective-permute-start | bytes 393224 | tf_op jit(solution)/shard_map/ppermute | solution.py:463
  45.9 8.8 %collective-permute-start.9 = (bf16[64,1024]{1,0:T(8,128)(2,1)S(1)}, bf16[64,1024]{1,0:T(8,128)(2,1)S(1)}, u32[]{:S(2)}, u32[]{:S(2)}) collective-permute-start(bf16[64,1024]{1,0:T(8,128)(2,1)S(1)} %get-tuple-element.40), channel_id=1, source_target_pairs={{0,1},{1,2},{2,3},{3,0},{4,5},{5,6},{6,7},{7,4},{8,9},{9,10},{10,1... | collective-permute-start | bytes 393224 | tf_op jit(solution)/shard_map/ppermute | solution.py:463
  61.9 36.3 %collective-permute-start.10 = (bf16[2,256,1024]{2,1,0:T(8,128)(2,1)S(1)}, bf16[2,256,1024]{2,1,0:T(8,128)(2,1)S(1)}, u32[]{:S(2)}, u32[]{:S(2)}) collective-permute-start(bf16[2,256,1024]{2,1,0:T(8,128)(2,1)S(1)} %get-tuple-element.44), channel_id=1, source_target_pairs={{0,4},{4,8},{8,12},{12,16},{16,20},{20,24},{24,28},{28,32},{32,36}... | collective-permute-start | bytes 3145736 | tf_op jit(solution)/shard_map/ppermute | solution.py:487
  65.9 32.3 %collective-permute-start.11 = (bf16[2,256,1024]{2,1,0:T(8,128)(2,1)S(1)}, bf16[2,256,1024]{2,1,0:T(8,128)(2,1)S(1)}, u32[]{:S(2)}, u32[]{:S(2)}) collective-permute-start(bf16[2,256,1024]{2,1,0:T(8,128)(2,1)S(1)} %get-tuple-element.45), channel_id=1, source_target_pairs={{0,252},{4,0},{8,4},{12,8},{16,12},{20,16},{24,20},{28,24},{32,28}... | collective-permute-start | bytes 3145736 | tf_op jit(solution)/shard_map/ppermute | solution.py:486
  65.9 7.6 %collective-permute-start.12 = (bf16[64,1024]{1,0:T(8,128)(2,1)S(1)}, bf16[64,1024]{1,0:T(8,128)(2,1)S(1)}, u32[]{:S(2)}, u32[]{:S(2)}) collective-permute-start(bf16[64,1024]{1,0:T(8,128)(2,1)S(1)} %get-tuple-element.48), channel_id=1, source_target_pairs={{0,3},{1,0},{2,1},{3,2},{4,7},{5,4},{6,5},{7,6},{8,11},{9,8},{10,9... | collective-permute-start | bytes 393224 | tf_op jit(solution)/shard_map/ppermute | solution.py:463
  67.8 6.8 %collective-permute-start.13 = (bf16[64,1024]{1,0:T(8,128)(2,1)S(1)}, bf16[64,1024]{1,0:T(8,128)(2,1)S(1)}, u32[]{:S(2)}, u32[]{:S(2)}) collective-permute-start(bf16[64,1024]{1,0:T(8,128)(2,1)S(1)} %get-tuple-element.49), channel_id=1, source_target_pairs={{0,2},{1,3},{2,0},{3,1},{4,6},{5,7},{6,4},{7,5},{8,10},{9,11},{10,... | collective-permute-start | bytes 393224 | tf_op jit(solution)/shard_map/ppermute | solution.py:463
  69.8 7.1 %collective-permute-start.14 = (bf16[64,1024]{1,0:T(8,128)(2,1)S(1)}, bf16[64,1024]{1,0:T(8,128)(2,1)S(1)}, u32[]{:S(2)}, u32[]{:S(2)}) collective-permute-start(bf16[64,1024]{1,0:T(8,128)(2,1)S(1)} %get-tuple-element.50), channel_id=1, source_target_pairs={{0,1},{1,2},{2,3},{3,0},{4,5},{5,6},{6,7},{7,4},{8,9},{9,10},{10,1... | collective-permute-start | bytes 393224 | tf_op jit(solution)/shard_map/ppermute | solution.py:463
  81.9 7.8 %collective-permute-start.15 = (bf16[2,64,1024]{2,1,0:T(8,128)(2,1)S(1)}, bf16[2,64,1024]{2,1,0:T(8,128)(2,1)S(1)}, u32[]{:S(2)}, u32[]{:S(2)}) collective-permute-start(bf16[2,64,1024]{2,1,0:T(8,128)(2,1)S(1)} %get-tuple-element.52), channel_id=1, source_target_pairs={{0,3},{1,0},{2,1},{3,2},{4,7},{5,4},{6,5},{7,6},{8,11},{9,8},{10,9... | collective-permute-start | bytes 786440 | tf_op jit(solution)/shard_map/ppermute | solution.py:463
  82.9 8.9 %collective-permute-start.16 = (bf16[2,64,1024]{2,1,0:T(8,128)(2,1)S(1)}, bf16[2,64,1024]{2,1,0:T(8,128)(2,1)S(1)}, u32[]{:S(2)}, u32[]{:S(2)}) collective-permute-start(bf16[2,64,1024]{2,1,0:T(8,128)(2,1)S(1)} %get-tuple-element.53), channel_id=1, source_target_pairs={{0,2},{1,3},{2,0},{3,1},{4,6},{5,7},{6,4},{7,5},{8,10},{9,11},{10,... | collective-permute-start | bytes 786440 | tf_op jit(solution)/shard_map/ppermute | solution.py:463
  82.9 15.3 %collective-permute-start.17 = (bf16[2,64,1024]{2,1,0:T(8,128)(2,1)S(1)}, bf16[2,64,1024]{2,1,0:T(8,128)(2,1)S(1)}, u32[]{:S(2)}, u32[]{:S(2)}) collective-permute-start(bf16[2,64,1024]{2,1,0:T(8,128)(2,1)S(1)} %get-tuple-element.54), channel_id=1, source_target_pairs={{0,1},{1,2},{2,3},{3,0},{4,5},{5,6},{6,7},{7,4},{8,9},{9,10},{10,1... | collective-permute-start | bytes 786440 | tf_op jit(solution)/shard_map/ppermute | solution.py:463
where the time goes:
time: 101 us; the launch traced here: 100 us
  Pallas kernels  34.8 us (34%)
  starting transfers between devices  30.9 us (31%)
  waiting for transfers between devices  30.4 us (30%)
  local copies, waits for them, and re-layouts  3.45 us (3%)
    ppermute x12, waiting for transfers between devices, shift(): return lax.ppermute(x, 'tm', [(i, (i + d) % steps) for i in range(steps)])  30.3 us
    ppermute x2, starting transfers between devices, body(): k_low, v_low = (lax.ppermute(k, 'space', up), lax.ppermute(v, 'space', up))  14.4 us
    ppermute x12, starting transfers between devices, shift(): return lax.ppermute(x, 'tm', [(i, (i + d) % steps) for i in range(steps)])  11.2 us
    pallas_call x1, Pallas kernels, window_forward(): pl.pallas_call(forward_kernel, in_specs=[SMEM_SPEC] * 3 + [VMEM_SPEC] * 8...  8.16 us
    pallas_call x1, Pallas kernels, back_sides(): pl.pallas_call(back_sides_kernel, in_specs=[SMEM_SPEC] * 2 + [VMEM_SPEC]...  7.16 us
    pallas_call x1, Pallas kernels, back_own(): pl.pallas_call(back_own_kernel, in_specs=[SMEM_SPEC] + [VMEM_SPEC] * 10,...  6.01 us
    pallas_call x1, Pallas kernels, time_first(): pl.pallas_call(time_first_kernel, grid_spec=pltpu.PrefetchScalarGridSpec(...  5.01 us
    pallas_call x1, Pallas kernels, time_second(): pl.pallas_call(time_second_kernel, grid_spec=pltpu.PrefetchScalarGridSpec...  4.97 us
  transfers between devices with their start and end apart: 18, of which 8 were waited for; matrix products, arithmetic and copies ran while one was open for 0% of the time, Pallas kernels for 24%

commit v1 on v0

v1 whole, which is shorter than its diff:
```python
import functools

import jax
import jax.numpy as jnp
from jax import lax
from jax.experimental import pallas as pl
from jax.experimental.pallas import tpu as pltpu
from jax.sharding import PartitionSpec as P

BLOCK = 128
H = 16
HD = 64
D = 1024
TOK = 256
QUARTER = 64
PAIRS = 8
SCALE = HD**-0.5
NEG = -1e30
F32 = jnp.float32
BF16 = jnp.bfloat16

VMEM_SPEC = pl.BlockSpec(memory_space=pltpu.VMEM)
ANY_SPEC = pl.BlockSpec(memory_space=pl.ANY)
HBM_SPEC = pl.BlockSpec(memory_space=pltpu.MemorySpace.HBM)
SMEM_SPEC = pl.BlockSpec(memory_space=pltpu.SMEM)


def dot(a, b):
    return jnp.dot(a, b, preferred_element_type=F32)


def kernel_params(mib):
    return pltpu.CompilerParams(vmem_limit_bytes=mib * 1024 * 1024)


def cost(flops, nbytes):
    return pl.CostEstimate(flops=flops, bytes_accessed=nbytes, transcendentals=0)


def transposed(block):
    return block.astype(F32).T.astype(BF16)


def head_rows(block):
    row = lax.broadcasted_iota(jnp.int32, block.shape, 0)
    zero = jnp.zeros_like(block)
    return jnp.where(row < HD, block, zero), jnp.where(row < HD, zero, block)


def head_lanes(block):
    lane = lax.broadcasted_iota(jnp.int32, block.shape, 1)
    zero = jnp.zeros_like(block)
    return jnp.where(lane < HD, block, zero), jnp.where(lane < HD, zero, block)


def grouped_lanes(block_t):
    first, second = head_rows(block_t)
    return jnp.concatenate(
        [first[:, :BLOCK], second[:, :BLOCK], first[:, BLOCK:], second[:, BLOCK:]], axis=1
    )


def grouped_rows(block):
    first, second = head_lanes(block)
    return jnp.concatenate([first[:BLOCK], second[:BLOCK], first[BLOCK:], second[BLOCK:]], axis=0)


def stage_kernel(place, qt, kt, og, k, v, m1, m2, m3, kv, small, large, sems_in, sems_out):
    copies = []
    for d, out in ((1, m1), (3, m3), (2, m2)):
        start = pl.multiple_of(lax.rem(place[0] + d, 4) * QUARTER, QUARTER)
        for a, array in enumerate((qt, kt, og)):
            copies.append((array.at[pl.ds(start, QUARTER), :], small.at[3 * d - 3 + a], out.at[a]))
    copies += [(k, large.at[0], kv.at[0]), (v, large.at[1], kv.at[1])]
    ins = [pltpu.make_async_copy(a, b, sems_in.at[i]) for i, (a, b, c) in enumerate(copies)]
    outs = [pltpu.make_async_copy(b, c, sems_out.at[i]) for i, (a, b, c) in enumerate(copies)]
    for copy in ins:
        copy.start()
    for copy, after in zip(ins, outs, strict=True):
        copy.wait()
        after.start()
    for copy in outs:
        copy.wait()


def stage(place, *arrays):
    piece = jax.ShapeDtypeStruct((3, QUARTER, D), BF16)
    return pl.pallas_call(
        stage_kernel,
        in_specs=[SMEM_SPEC] + [HBM_SPEC] * 5,
        out_specs=[HBM_SPEC] * 4,
        out_shape=[piece] * 3 + [jax.ShapeDtypeStruct((2, TOK, D), BF16)],
        scratch_shapes=[
            pltpu.VMEM((9, QUARTER, D), BF16),
            pltpu.VMEM((2, TOK, D), BF16),
            pltpu.SemaphoreType.DMA((11,)),
            pltpu.SemaphoreType.DMA((11,)),
        ],
        compiler_params=kernel_params(60),
        cost_estimate=cost(0, 4 << 20),
        name="stage",
    )(place, *arrays)


def listed(place, lists, side):
    return [lists[b * 4 + 2 + side] for b in range(2)]


def neighbour_rows(low_ref, high_ref, low_ids, high_ids, b, lanes):
    low = low_ref[pl.ds(pl.multiple_of(low_ids[b] * BLOCK, BLOCK), BLOCK), lanes]
    high = high_ref[pl.ds(pl.multiple_of(high_ids[b] * BLOCK, BLOCK), BLOCK), lanes]
    return jnp.concatenate([low, high], axis=0)


def dead_column(occ, row_id, keep):
    dead = occ[pl.ds(row_id, 1), :].astype(F32)
    row = jnp.where((dead > 0.5) | jnp.logical_not(keep), NEG, 0.0)
    return jnp.broadcast_to(row, (BLOCK, BLOCK)).T


def pair_slice(p):
    return pl.ds(pl.multiple_of(p * 128, 128), 128)


def forward_own_kernel(place, fluid, occ, q, k, v, weights, stats, partial, bias):
    dom = place[1]
    for b in range(2):
        keep = fluid[dom * 2 + b] > 0
        for n in range(2):
            bias[b, n * 128 : n * 128 + 128] = dead_column(occ, dom * 2 + n, keep)

    def pair(p):
        lanes = pair_slice(p)
        q_cols = grouped_lanes((q[:, lanes].astype(F32) * SCALE).T.astype(BF16))
        v_t = transposed(v[:, lanes])
        scores = dot(k[:, lanes], q_cols)
        outs = []
        for g in range(4):
            cols = slice(g * 128, g * 128 + 128)
            s = scores[:, cols] + bias[g // 2]
            m = jnp.maximum(jnp.max(s, axis=0, keepdims=True), 0.0)
            e = jnp.exp(s - m)
            stats[p, 0:1, cols] = m
            stats[p, 1:2, cols] = jnp.sum(e, axis=0, keepdims=True)
            e = e.astype(BF16)
            weights[p, :, cols] = e
            outs.append(dot(v_t[(g % 2) * HD : (g % 2) * HD + HD], e))
        partial[pair_slice(p), :] = jnp.concatenate(
            [jnp.concatenate(outs[:2], axis=0), jnp.concatenate(outs[2:], axis=0)], axis=1
        )

    pl.loop(0, PAIRS, unroll=8)(pair)


def forward_own(place, fluid, occ, q, k, v):
    return pl.pallas_call(
        forward_own_kernel,
        in_specs=[SMEM_SPEC] * 2 + [VMEM_SPEC] * 4,
        out_specs=[VMEM_SPEC] * 3,
        out_shape=[
            jax.ShapeDtypeStruct((PAIRS, TOK, 512), BF16),
            jax.ShapeDtypeStruct((PAIRS, 8, 512), F32),
            jax.ShapeDtypeStruct((D, TOK), F32),
        ],
        scratch_shapes=[pltpu.VMEM((2, TOK, BLOCK), F32)],
        compiler_params=kernel_params(24),
        cost_estimate=cost(2_000_000_000, 8 << 20),
        name="forward_own",
    )(place, fluid, occ, q, k, v)


def forward_sides_kernel(
    place, lists, fluid, occ, q, low, high, stats, partial,
    states, p1, p2, p3, probs, states_t, factors, bias, scratch,
):
    me, dom = place[0], place[1]
    low_dom, high_dom = lax.rem(dom + 63, 64), lax.rem(dom + 1, 64)
    low_ids, high_ids = listed(place, lists, 0), listed(place, lists, 1)
    for b in range(2):
        keep = fluid[dom * 2 + b] > 0
        for h in (slice(0, 128), slice(128, 256)):
            bias[b, 0:128, h] = dead_column(occ, low_dom * 2 + low_ids[b], keep)
            bias[b, 128:256, h] = dead_column(occ, high_dom * 2 + high_ids[b], keep)

    def pair(p):
        lanes = pair_slice(p)
        q_cols = grouped_lanes((q[:, lanes].astype(F32) * SCALE).T.astype(BF16))
        outs = []
        for b in range(2):
            k_n = neighbour_rows(low.at[0], high.at[0], low_ids, high_ids, b, lanes)
            v_t = transposed(neighbour_rows(low.at[1], high.at[1], low_ids, high_ids, b, lanes))
            scores = dot(k_n, q_cols[:, 256 * b : 256 * b + 256])
            cols = slice(256 * b, 256 * b + 256)
            s = scores + bias[b]
            m_own, l_own = stats[p, 0:1, cols], stats[p, 1:2, cols]
            m = jnp.maximum(jnp.max(s, axis=0, keepdims=True), m_own)
            e = jnp.exp(s - m)
            scale_own = jnp.exp(m_own - m)
            total = jnp.exp(-m) + scale_own * l_own + jnp.sum(e, axis=0, keepdims=True)
            inv = 1.0 / total
            own = scale_own * inv
            factors[p, 0:1, cols] = own
            pr = (e * inv).astype(BF16)
            probs[p, :, cols] = pr
            halves = []
            for h in range(2):
                rows = pl.ds(pl.multiple_of(p * 128 + h * HD, HD), HD)
                half = slice(h * 128, h * 128 + 128)
                halves.append(
                    dot(v_t[h * HD : h * HD + HD], pr[:, half])
                    + partial[rows, b * 128 : b * 128 + 128] * own[:, half]
                )
            outs.append(jnp.concatenate(halves, axis=0))
        out_t = jnp.concatenate(outs, axis=1)
        states_t[pair_slice(p), :] = out_t.astype(BF16)
        scratch[:, lanes] = out_t.T.astype(BF16)

    pl.loop(0, PAIRS, unroll=8)(pair)
    for d, piece in ((0, states), (1, p1), (2, p2), (3, p3)):
        start = pl.multiple_of(lax.rem(me + d, 4) * QUARTER, QUARTER)
        piece[...] = scratch[pl.ds(start, QUARTER), :]


def forward_sides(place, lists, fluid, occ, q, low, high, stats, partial):
    piece = jax.ShapeDtypeStruct((QUARTER, D), BF16)
    return pl.pallas_call(
        forward_sides_kernel,
        in_specs=[SMEM_SPEC] * 3 + [VMEM_SPEC] * 6,
        out_specs=[VMEM_SPEC] * 7,
        out_shape=[piece] * 4
        + [
            jax.ShapeDtypeStruct((PAIRS, TOK, 512), BF16),
            jax.ShapeDtypeStruct((D, TOK), BF16),
            jax.ShapeDtypeStruct((PAIRS, 8, 512), F32),
        ],
        scratch_shapes=[pltpu.VMEM((2, TOK, TOK), F32), pltpu.VMEM((TOK, D), BF16)],
        compiler_params=kernel_params(24),
        cost_estimate=cost(2_000_000_000, 8 << 20),
        name="forward_sides",
    )(place, lists, fluid, occ, q, low, high, stats, partial)


ROWS = 16
WIDE = 256


def head_sums():
    row = lax.broadcasted_iota(jnp.int32, (2 * WIDE, WIDE), 0) % WIDE
    lane = lax.broadcasted_iota(jnp.int32, (2 * WIDE, WIDE), 1)
    return jnp.where(row // HD == lane // HD, 1.0, 0.0).astype(BF16)


def pair_sums(left, right, ones):
    products = jnp.concatenate([a * b for a in left for b in right], axis=0)
    high = products.astype(BF16)
    low = (products - high.astype(F32)).astype(BF16)
    sums = dot(jnp.concatenate([high, low], axis=1), ones)
    return [[sums[(4 * t + u) * ROWS : (4 * t + u + 1) * ROWS] for u in range(4)] for t in range(4)]


def time_first_kernel(place, q0, k0, g0, m1, m2, m3, after, s0, s1, s2, s3, attn, ones_ref):
    ones_ref[...] = head_sums()
    outs = (s0, s1, s2, s3)

    def tile(i):
        rows = pl.ds(pl.multiple_of((i // 4) * ROWS, ROWS), ROWS)
        lanes = pl.ds(pl.multiple_of((i % 4) * WIDE, WIDE), WIDE)
        here = pl.ds(pl.multiple_of(place[0] * QUARTER + (i // 4) * ROWS, ROWS), ROWS)
        qs = [x.astype(F32) for x in (q0[here, lanes], *(m[0, rows, lanes] for m in (m1, m2, m3)))]
        ks = [x.astype(F32) for x in (k0[here, lanes], *(m[1, rows, lanes] for m in (m1, m2, m3)))]
        gs = [x.astype(F32) for x in (g0[here, lanes], *(m[2, rows, lanes] for m in (m1, m2, m3)))]
        scores = pair_sums([x * SCALE for x in qs], ks, ones_ref[...])
        sums = list(gs)
        for t in range(4):
            row = scores[t]
            top = jnp.maximum(jnp.maximum(row[0], row[1]), jnp.maximum(row[2], row[3]))
            exps = [jnp.exp(x - top) for x in row]
            inv = 1.0 / ((exps[0] + exps[1]) + (exps[2] + exps[3]))
            for u in range(4):
                a = exps[u] * inv
                attn[4 * t + u, rows, lanes] = a.astype(BF16)
                sums[u] = sums[u] + a * gs[t]
        for u in range(4):
            outs[u][rows, lanes] = sums[u].astype(BF16)

    pl.loop(0, 16, unroll=4)(tile)


def time_first(place, q, k, g, m1, m2, m3, after):
    piece = jax.ShapeDtypeStruct((QUARTER, D), BF16)
    return pl.pallas_call(
        time_first_kernel,
        in_specs=[SMEM_SPEC] + [VMEM_SPEC] * 6 + [ANY_SPEC],
        out_specs=[VMEM_SPEC] * 5,
        out_shape=[piece] * 4 + [jax.ShapeDtypeStruct((16, QUARTER, D), BF16)],
        scratch_shapes=[pltpu.VMEM((2 * WIDE, WIDE), BF16)],
        compiler_params=kernel_params(24),
        cost_estimate=cost(1_000_000_000, 8 << 20),
        name="time_first",
    )(place, q, k, g, m1, m2, m3, after)


def time_second_kernel(
    place, q0, k0, g0, m1, m2, m3, attn, x0, x1, x2, x3, o0, o1, o2, o3, ones_ref
):
    ones_ref[...] = head_sums()
    outs = (o0, o1, o2, o3)

    def tile(i):
        rows = pl.ds(pl.multiple_of((i // 4) * ROWS, ROWS), ROWS)
        lanes = pl.ds(pl.multiple_of((i % 4) * WIDE, WIDE), WIDE)
        here = pl.ds(pl.multiple_of(place[0] * QUARTER + (i // 4) * ROWS, ROWS), ROWS)
        gs = [x.astype(F32) for x in (g0[here, lanes], *(m[2, rows, lanes] for m in (m1, m2, m3)))]
        xs = [x[rows, lanes].astype(F32) for x in (x0, x1, x2, x3)]
        dattn = pair_sums(gs, xs, ones_ref[...])
        qs = [x.astype(F32) for x in (q0[here, lanes], *(m[0, rows, lanes] for m in (m1, m2, m3)))]
        ks = [x.astype(F32) for x in (k0[here, lanes], *(m[1, rows, lanes] for m in (m1, m2, m3)))]
        key_sums = [None] * 4
        for t in range(4):
            a = [attn[4 * t + u, rows, lanes].astype(F32) for u in range(4)]
            mean = sum(x * y for x, y in zip(a[1:], dattn[t][1:], strict=True)) + a[0] * dattn[t][0]
            query_sum = None
            for u in range(4):
                grad = a[u] * (dattn[t][u] - mean)
                query_sum = grad * ks[u] if query_sum is None else query_sum + grad * ks[u]
                term = grad * qs[t]
                key_sums[u] = term if key_sums[u] is None else key_sums[u] + term
            outs[t][0, rows, lanes] = (query_sum * SCALE).astype(BF16)
        for u in range(4):
            outs[u][1, rows, lanes] = (key_sums[u] * SCALE).astype(BF16)

    pl.loop(0, 16, unroll=4)(tile)


def time_second(place, q, k, g, m1, m2, m3, attn, x0, x1, x2, x3):
    piece = jax.ShapeDtypeStruct((2, QUARTER, D), BF16)
    return pl.pallas_call(
        time_second_kernel,
        in_specs=[SMEM_SPEC] + [VMEM_SPEC] * 11,
        out_specs=[VMEM_SPEC] * 4,
        out_shape=[piece] * 4,
        scratch_shapes=[pltpu.VMEM((2 * WIDE, WIDE), BF16)],
        compiler_params=kernel_params(24),
        cost_estimate=cost(1_000_000_000, 8 << 20),
        name="time_second",
    )(place, q, k, g, m1, m2, m3, attn, x0, x1, x2, x3)


def grad_rows(sg, place, pieces):
    for d, piece in enumerate(pieces):
        start = pl.multiple_of(lax.rem(place[0] + d, 4) * QUARTER, QUARTER)
        sg[pl.ds(start, QUARTER), :] = piece[...]


def deltas(sg_t, st_t):
    product = sg_t.astype(F32) * st_t.astype(F32)
    first = jnp.sum(product[:HD], axis=0, keepdims=True)
    second = jnp.sum(product[HD:], axis=0, keepdims=True)
    return jnp.concatenate(
        [first[:, :BLOCK], second[:, :BLOCK], first[:, BLOCK:], second[:, BLOCK:]], axis=1
    )


def back_sides_kernel(
    place, lists, q, from_low, from_high, probs, states_t, g0, g1, g2, g3, after,
    to_low, to_high, query_part, sg,
):
    low_ids, high_ids = listed(place, lists, 0), listed(place, lists, 1)
    grad_rows(sg, place, (g0, g1, g2, g3))

    def pair(p):
        lanes = pl.ds(pl.multiple_of(p * 128, 128), 128)
        rows = pl.ds(pl.multiple_of(p * 128, 128), 128)
        sg_p = sg[:, lanes]
        sg_t = transposed(sg_p)
        sg_cols, sg_rows, q_rows = grouped_lanes(sg_t), grouped_rows(sg_p), grouped_rows(q[:, lanes])
        delta = deltas(sg_t, states_t[rows, :])
        key_parts, value_parts = [], []
        for b in range(2):
            cols = slice(256 * b, 256 * b + 256)
            k_n = neighbour_rows(from_low.at[0], from_high.at[0], low_ids, high_ids, b, lanes)
            v_n = neighbour_rows(from_low.at[1], from_high.at[1], low_ids, high_ids, b, lanes)
            k_n_t = transposed(k_n)
            dp = dot(v_n, sg_cols[:, cols])
            pr = probs[p, :, cols]
            ds = (pr.astype(F32) * (dp - delta[:, cols])).astype(BF16)
            query_part[rows, b * 128 : b * 128 + 128] = jnp.concatenate(
                [dot(k_n_t[:HD], ds[:, :BLOCK]), dot(k_n_t[HD:], ds[:, BLOCK:])], axis=0
            )
            key_parts.append(dot(ds, q_rows[cols]) * SCALE)
            value_parts.append(dot(pr, sg_rows[cols]))
        for n, parts in enumerate((key_parts, value_parts)):
            for ids, out, side in ((low_ids, to_low, 0), (high_ids, to_high, 1)):
                for j in range(2):
                    total = sum(
                        jnp.where(ids[b] == j, parts[b][side * 128 : side * 128 + 128], 0.0)
                        for b in range(2)
                    )
                    out[n, j * 128 : j * 128 + 128, lanes] = total.astype(BF16)

    pl.loop(0, PAIRS, unroll=8)(pair)


def back_sides(place, lists, q, low, high, probs, states_t, pieces, after):
    message = jax.ShapeDtypeStruct((2, TOK, D), BF16)
    return pl.pallas_call(
        back_sides_kernel,
        in_specs=[SMEM_SPEC] * 2 + [VMEM_SPEC] * 9 + [ANY_SPEC],
        out_specs=[VMEM_SPEC] * 3,
        out_shape=[message, message, jax.ShapeDtypeStruct((D, TOK), F32)],
        scratch_shapes=[pltpu.VMEM((TOK, D), BF16)],
        compiler_params=kernel_params(32),
        cost_estimate=cost(6_000_000_000, 16 << 20),
        name="back_sides",
    )(place, lists, q, low, high, probs, states_t, *pieces, after)


def back_own_kernel(
    place, q, k, v, weights, factors, states_t, query_part, g0, g1, g2, g3, query_grad, totals, sg
):
    grad_rows(sg, place, (g0, g1, g2, g3))

    def pair(p):
        lanes = pl.ds(pl.multiple_of(p * 128, 128), 128)
        rows = pl.ds(pl.multiple_of(p * 128, 128), 128)
        sg_p = sg[:, lanes]
        sg_t = transposed(sg_p)
        q_rows = grouped_rows(q[:, lanes])
        factor = factors[p, 0:1, :]
        delta = deltas(sg_t, states_t[rows, :]) * factor
        scaled = grouped_lanes(sg_t).astype(F32) * factor
        sg_cols, sg_rows = scaled.astype(BF16), scaled.T.astype(BF16)
        k_t = transposed(k[:, lanes])
        dp = dot(v[:, lanes], sg_cols)
        pr = weights[p]
        ds = (pr.astype(F32) * (dp - delta)).astype(BF16)
        cols = [
            jnp.concatenate(
                [
                    dot(k_t[:HD], ds[:, 256 * b : 256 * b + 128]),
                    dot(k_t[HD:], ds[:, 256 * b + 128 : 256 * b + 256]),
                ],
                axis=0,
            )
            for b in range(2)
        ]
        query_t = jnp.concatenate(cols, axis=1) + query_part[rows, :]
        query_grad[:, lanes] = (query_t * SCALE).T.astype(BF16)
        totals[0, :, lanes] = dot(ds, q_rows) * SCALE
        totals[1, :, lanes] = dot(pr, sg_rows)

    pl.loop(0, PAIRS, unroll=8)(pair)


def back_own(place, q, k, v, weights, factors, states_t, query_part, pieces):
    return pl.pallas_call(
        back_own_kernel,
        in_specs=[SMEM_SPEC] + [VMEM_SPEC] * 11,
        out_specs=[VMEM_SPEC] * 2,
        out_shape=[
            jax.ShapeDtypeStruct((TOK, D), BF16),
            jax.ShapeDtypeStruct((2, TOK, D), F32),
        ],
        scratch_shapes=[pltpu.VMEM((TOK, D), BF16)],
        compiler_params=kernel_params(32),
        cost_estimate=cost(6_000_000_000, 16 << 20),
        name="back_own",
    )(place, q, k, v, weights, factors, states_t, query_part, *pieces)


def finish_time_kernel(place, t0, t1, t2, t3, query_t, key_t):
    for d, piece in enumerate((t0, t1, t2, t3)):
        start = pl.multiple_of(lax.rem(place[0] + d, 4) * QUARTER, QUARTER)
        query_t[pl.ds(start, QUARTER), :] = piece[0]
        key_t[pl.ds(start, QUARTER), :] = piece[1]


def finish_time(place, pieces):
    return pl.pallas_call(
        finish_time_kernel,
        in_specs=[SMEM_SPEC] + [VMEM_SPEC] * 4,
        out_specs=[VMEM_SPEC] * 2,
        out_shape=[jax.ShapeDtypeStruct((TOK, D), BF16)] * 2,
        compiler_params=kernel_params(24),
        cost_estimate=cost(0, 2 << 20),
        name="finish_time",
    )(place, *pieces)


def finish_kernel(totals, low, high, key_grad, value_grad):
    for n, out in ((0, key_grad), (1, value_grad)):
        out[...] = (totals[n] + low[n].astype(F32) + high[n].astype(F32)).astype(BF16)


def finish(totals, low, high):
    return pl.pallas_call(
        finish_kernel,
        in_specs=[VMEM_SPEC] * 3,
        out_specs=[VMEM_SPEC] * 2,
        out_shape=[jax.ShapeDtypeStruct((TOK, D), BF16)] * 2,
        compiler_params=kernel_params(24),
        cost_estimate=cost(0, 5 << 20),
        name="finish",
    )(totals, low, high)


def body(
    queries, key_vectors, value_vectors, query_time, key_time, out_grad, fluid_mask, occupancy, key_lists
):
    q, k, v = queries[0], key_vectors[0], value_vectors[0]
    qt, kt, og = query_time[0], key_time[0], out_grad[0]
    me, dom = lax.axis_index("tm"), lax.axis_index("space")
    place = jnp.stack([me, dom]).astype(jnp.int32)
    lists = lax.dynamic_index_in_dim(key_lists, dom, 0, keepdims=False)[:, :, 1].reshape(-1)
    occ = occupancy.reshape(-1, BLOCK)

    domains, steps = lax.axis_size("space"), lax.axis_size("tm")
    up = [(i, (i + 1) % domains) for i in range(domains)]
    down = [(i, (i - 1) % domains) for i in range(domains)]

    def shift(x, d):
        return lax.ppermute(x, "tm", [(i, (i + d) % steps) for i in range(steps)])

    m1, m2, m3, kv = stage(place, qt, kt, og, k, v)
    sent = (None, m1, m2, m3)
    arrived = {(4 - d) % 4: shift(sent[d], d) for d in (1, 3, 2)}
    ms = (arrived[1], arrived[2], arrived[3])
    low, high = lax.ppermute(kv, "space", up), lax.ppermute(kv, "space", down)

    weights, stats, partial = forward_own(place, fluid_mask, occ, q, k, v)
    *pieces, probs, states_t, factors = forward_sides(
        place, lists, fluid_mask, occ, q, low, high, stats, partial
    )
    *grads, attn = time_first(place, qt, kt, og, *ms, pieces[0])
    home = {(4 - d) % 4: shift(grads[d], d) for d in (1, 3, 2)}
    grad_pieces = (grads[0], home[1], home[2], home[3])

    there = {(4 - d) % 4: shift(pieces[d], d) for d in (1, 3, 2)}
    back = time_second(place, qt, kt, og, *ms, attn, pieces[0], there[1], there[2], there[3])

    to_low, to_high, query_part = back_sides(
        place, lists, q, low, high, probs, states_t, grad_pieces, back[0]
    )
    from_high = lax.ppermute(to_low, "space", down)
    from_low = lax.ppermute(to_high, "space", up)
    returned = {(4 - d) % 4: shift(back[d], d) for d in (1, 3, 2)}
    query_time_grad, key_time_grad = finish_time(
        place, (back[0], returned[1], returned[2], returned[3])
    )
    query_grad, totals = back_own(
        place, q, k, v, weights, factors, states_t, query_part, grad_pieces
    )
    key_grad, value_grad = finish(totals, from_low, from_high)
    return tuple(
        x[None] for x in (query_grad, key_grad, value_grad, query_time_grad, key_time_grad)
    )


def solution(mesh):
    split = P("tm", "space", None)
    return jax.shard_map(
        body,
        mesh=mesh,
        in_specs=(split,) * 6 + (P(),) * 3,
        out_specs=(split,) * 5,
        check_vma=False,
    )
```

time: 101 us -> 74.4 us (0.74)
  waiting for transfers between devices: 30.4 us -> 16.6 us
  starting transfers between devices: 30.9 us -> 19.6 us
  local copies, waits for them, and re-layouts: 3.45 us -> 1.38 us
    ppermute x12, waiting for transfers between devices: 30.3 us -> 9.49 us  [shift(): return lax.ppermute(x, 'tm', [(i, (i + d) % steps) for i in range(steps)])]
    ppermute x4 -> x2, starting transfers between devices: 15.7 us -> 3.49 us  [body(): low, high = (lax.ppermute(kv, 'space', up), lax.ppermute(kv, 'space', down))]
    ppermute x4 -> x2, waiting for transfers between devices: 0.01 us -> 7.13 us  [body(): low, high = (lax.ppermute(kv, 'space', up), lax.ppermute(kv, 'space', down))]
    ppermute x12, starting transfers between devices: 11.2 us -> 13.3 us  [shift(): return lax.ppermute(x, 'tm', [(i, (i + d) % steps) for i in range(steps)])]
    unnamed x20 -> x22, local copies, waits for them, and re-layouts: 3.16 us -> 1.09 us
    ppermute x1, starting transfers between devices: 4.04 us -> 2.86 us  [body(): from_low = lax.ppermute(to_high, 'space', up)]
    pallas_call x6 -> x8, Pallas kernels: 27.6 us -> 28.3 us  [the longest x1 6.62 us: forward_sides(): pl.pallas_call(forward_sides_kernel, in_specs=[SMEM_SPEC] * 3 + [VMEM_SPE...]
  transfers between devices with their start and end apart: 18 -> 16, of which waited for: 8 -> 7; matrix products, arithmetic and copies ran while one was open for 0% -> 0% of each run, Pallas kernels for 24% -> 32%
where the time goes in v1:
time: 74.4 us; the launch traced here: 73.6 us
  Pallas kernels  34.5 us (46%)
  starting transfers between devices  19.6 us (26%)
  waiting for transfers between devices  16.6 us (22%)
  local copies, waits for them, and re-layouts  1.38 us (2%)
  between operations  0.82 us (1%)
    ppermute x12, starting transfers between devices, shift(): return lax.ppermute(x, 'tm', [(i, (i + d) % steps) for i in range(steps)])  13.3 us
    ppermute x12, waiting for transfers between devices, shift(): return lax.ppermute(x, 'tm', [(i, (i + d) % steps) for i in range(steps)])  9.49 us
    ppermute x2, waiting for transfers between devices, body(): low, high = (lax.ppermute(kv, 'space', up), lax.ppermute(kv, 'space', down))  7.13 us
    pallas_call x1, Pallas kernels, forward_sides(): pl.pallas_call(forward_sides_kernel, in_specs=[SMEM_SPEC] * 3 + [VMEM_SPE...  6.62 us
    pallas_call x1, Pallas kernels, back_sides(): pl.pallas_call(back_sides_kernel, in_specs=[SMEM_SPEC] * 2 + [VMEM_SPEC]...  6.23 us
    pallas_call x1, Pallas kernels, back_own(): pl.pallas_call(back_own_kernel, in_specs=[SMEM_SPEC] + [VMEM_SPEC] * 11,...  4.88 us
    pallas_call x1, Pallas kernels, forward_own(): pl.pallas_call(forward_own_kernel, in_specs=[SMEM_SPEC] * 2 + [VMEM_SPEC]...  3.64 us
    ppermute x2, starting transfers between devices, body(): low, high = (lax.ppermute(kv, 'space', up), lax.ppermute(kv, 'space', down))  3.49 us
  transfers between devices with their start and end apart: 16, of which 7 were waited for; matrix products, arithmetic and copies ran while one was open for 0% of the time, Pallas kernels for 32%

profile of v1, /device:TPU:103, one launch (start us, length us, event | category | flops | bytes accessed | tf_op | source)
XLA Modules:
  0.0 73.6 jit_solution(13309073327685161444)
XLA Ops:
  0.6 0.0 copy-start
  0.6 0.0 copy-start.4
  0.7 0.0 copy-start.5
  0.7 0.0 copy-start.10
  0.7 0.0 copy-start.9
  0.7 0.6 pad_add_fusion.place
  1.3 0.0 copy-start.6
  1.3 3.5 %stage.1 = (bf16[3,64,1024]{2,1,0:T(8,128)(2,1)}, bf16[3,64,1024]{2,1,0:T(8,128)(2,1)}, bf16[3,64,1024]{2,1,0:T(8,128)(2,1)}, bf16[2,256,1024]{2,1,0:T(8,128)(2,1)}) custom-call(s32[2]{0:T(128)} %pad_add_fusion.place, bf16[256,1024]{1,0:T(8,128)(2,1)} %bitcast.15, bf16[256,1024]{1,0:T(8,128)(2,1)} %bitcast.18, bf16[256,1024]{1,0:T(8,128)(2,1)} %bitcast.21, ...), custom_call_target="tpu_custom_call" | custom-call | bytes 4194304 | tf_op jit(solution)/shard_map/stage/pallas_call | solution.py:88
  4.8 3.5 %collective-permute-start = (bf16[2,256,1024]{2,1,0:T(8,128)(2,1)}, bf16[2,256,1024]{2,1,0:T(8,128)(2,1)S(1)}, u32[]{:S(2)}, u32[]{:S(2)}) collective-permute-start(bf16[2,256,1024]{2,1,0:T(8,128)(2,1)} %get-tuple-element.38), channel_id=1, source_target_pairs={{0,4},{4,8},{8,12},{12,16},{16,20},{20,24},{24,28},{28,32},{32,36}... | collective-permute-start | bytes 3145736 | tf_op jit(solution)/shard_map/ppermute | solution.py:528
  8.3 0.0 collective-permute-start.1
  8.3 2.7 %collective-permute-start.2 = (bf16[3,64,1024]{2,1,0:T(8,128)(2,1)}, bf16[3,64,1024]{2,1,0:T(8,128)(2,1)S(1)}, u32[]{:S(2)}, u32[]{:S(2)}) collective-permute-start(bf16[3,64,1024]{2,1,0:T(8,128)(2,1)} %get-tuple-element.44), channel_id=1, source_target_pairs={{0,3},{1,0},{2,1},{3,2},{4,7},{5,4},{6,5},{7,6},{8,11},{9,8},{10,9... | collective-permute-start | bytes 1179656 | tf_op jit(solution)/shard_map/ppermute | solution.py:522
  11.0 0.3 collective-permute-start.3
  11.3 0.7 collective-permute-start.4
  12.0 0.0 copy-done
  12.0 0.1 constant_dynamic-slice_fusion
  12.1 0.1 copy.14
  12.2 0.1 reshape_squeeze.3.lists
  12.3 0.0 copy-done.4
  12.3 0.0 copy-done.5
  12.3 0.0 copy-done.10
  12.3 0.0 copy-done.9
  12.4 0.0 copy-done.6
  12.4 0.0 copy-start.7
  12.4 1.0 %copy-done.7 = bf16[1,256,1024]{2,1,0:T(8,128)(2,1)S(1)} copy-done((bf16[1,256,1024]{2,1,0:T(8,128)(2,1)S(1)}, bf16[1,256,1024]{2,1,0:T(8,128)(2,1)}, u32[]{:S(2)}) %copy-start.7) | copy-done | bytes 524312
  13.4 3.6 %forward_own.1 = (bf16[8,256,512]{2,1,0:T(8,128)(2,1)S(1)}, f32[8,8,512]{2,1,0:T(8,128)S(1)}, f32[1024,256]{1,0:T(8,128)S(1)}) custom-call(s32[2]{0:T(128)S(1)} %copy-done.6, s32[128]{0:T(128)S(1)} %copy-done.10, s32[128,128]{1,0:T(8,128)S(1)} %bitcast.34, bf16[256,1024]{1,0:T(8,128)(2,1)S(1)} %bitcast.30, bf16[256,1024]{1,0:T(8,128)(2,1)S(1)} %bitcast.25, ...), custom_call_target="tpu_custom_call" | custom-call | flops 2000000000 | bytes 8388608 | tf_op jit(solution)/shard_map/forward_own/pallas_call | solution.py:156
  17.1 3.3 %collective-permute-done.low.from_low = bf16[2,256,1024]{2,1,0:T(8,128)(2,1)S(1)} collective-permute-done((bf16[2,256,1024]{2,1,0:T(8,128)(2,1)}, bf16[2,256,1024]{2,1,0:T(8,128)(2,1)S(1)}, u32[]{:S(2)}, u32[]{:S(2)}) %collective-permute-start) | collective-permute-done | bytes 1048608 | tf_op jit(solution)/shard_map/ppermute | solution.py:528
  20.3 3.9 %collective-permute-done.1.high.from_high = bf16[2,256,1024]{2,1,0:T(8,128)(2,1)} collective-permute-done((bf16[2,256,1024]{2,1,0:T(8,128)(2,1)}, bf16[2,256,1024]{2,1,0:T(8,128)(2,1)}, u32[]{:S(2)}, u32[]{:S(2)}) %collective-permute-start.1) | collective-permute-done | bytes 1048608 | tf_op jit(solution)/shard_map/ppermute | solution.py:528
  24.2 6.6 %forward_sides.1 = (bf16[64,1024]{1,0:T(8,128)(2,1)S(1)}, bf16[64,1024]{1,0:T(8,128)(2,1)S(1)}, bf16[64,1024]{1,0:T(8,128)(2,1)S(1)}, bf16[64,1024]{1,0:T(8,128)...) custom-call(s32[2]{0:T(128)S(1)} %copy-done.6, ...), custom_call_target="tpu_custom_call" | custom-call | flops 2000000000 | bytes 8388608 | tf_op jit(solution)/shard_map/forward_sides/pallas_call | solution.py:226
  30.8 2.8 %collective-permute-start.8 = (bf16[64,1024]{1,0:T(8,128)(2,1)S(1)}, bf16[64,1024]{1,0:T(8,128)(2,1)S(1)}, u32[]{:S(2)}, u32[]{:S(2)}) collective-permute-start(bf16[64,1024]{1,0:T(8,128)(2,1)S(1)} %get-tuple-element.53), channel_id=1, source_target_pairs={{0,3},{1,0},{2,1},{3,2},{4,7},{5,4},{6,5},{7,6},{8,11},{9,8},{10,9... | collective-permute-start | bytes 393224 | tf_op jit(solution)/shard_map/ppermute | solution.py:522
  33.6 0.3 collective-permute-start.9
  33.9 0.0 collective-permute-done.2.m1
  33.9 0.6 collective-permute-start.10
  34.5 0.0 collective-permute-done.3.m2
  34.5 0.0 collective-permute-done.4.m3
  34.5 0.0 copy-done.1
  34.5 0.0 copy-done.2
  34.5 0.0 copy-done.3
  34.5 3.4 %time_first.1 = (bf16[64,1024]{1,0:T(8,128)(2,1)S(1)}, bf16[64,1024]{1,0:T(8,128)(2,1)S(1)}, bf16[64,1024]{1,0:T(8,128)(2,1)S(1)}, bf16[64,1024]{1,0:T(8,128)(2,1)S(1)}, bf16[16,64,1024]{2,1,0:T(8,128)(2,1)S(1)}) custom-call(s32[2]{0:T(128)S(1)} %copy-done.6, bf16[256,1024]{1,0:T(8,128)(2,1)S(1)} %bitcast.16, bf16[256,1024]{1,0:T(8,128)(2,1)S(1)} %bitcast.19, ...), custom_call_target="tpu_custom_call" | custom-call | flops 1000000000 | bytes 8388608 | tf_op jit(solution)/shard_map/time_first/pallas_call | solution.py:291
  38.0 2.2 %collective-permute-start.5 = (bf16[64,1024]{1,0:T(8,128)(2,1)S(1)}, bf16[64,1024]{1,0:T(8,128)(2,1)S(1)}, u32[]{:S(2)}, u32[]{:S(2)}) collective-permute-start(bf16[64,1024]{1,0:T(8,128)(2,1)S(1)} %get-tuple-element.49), channel_id=1, source_target_pairs={{0,3},{1,0},{2,1},{3,2},{4,7},{5,4},{6,5},{7,6},{8,11},{9,8},{10,9... | collective-permute-start | bytes 393224 | tf_op jit(solution)/shard_map/ppermute | solution.py:522
  40.1 1.5 %collective-permute-start.6 = (bf16[64,1024]{1,0:T(8,128)(2,1)S(1)}, bf16[64,1024]{1,0:T(8,128)(2,1)S(1)}, u32[]{:S(2)}, u32[]{:S(2)}) collective-permute-start(bf16[64,1024]{1,0:T(8,128)(2,1)S(1)} %get-tuple-element.50), channel_id=1, source_target_pairs={{0,2},{1,3},{2,0},{3,1},{4,6},{5,7},{6,4},{7,5},{8,10},{9,11},{10,... | collective-permute-start | bytes 393224 | tf_op jit(solution)/shard_map/ppermute | solution.py:522
  41.7 0.0 collective-permute-done.8.x1
  41.7 0.0 collective-permute-start.7
  41.7 0.0 collective-permute-done.9.x2
  41.7 0.0 collective-permute-done.10.x3
  41.7 0.0 copy-start.8
  41.7 3.4 %time_second.1 = (bf16[2,64,1024]{2,1,0:T(8,128)(2,1)S(1)}, bf16[2,64,1024]{2,1,0:T(8,128)(2,1)S(1)}, bf16[2,64,1024]{2,1,0:T(8,128)(2,1)S(1)}, bf16[2,64,1024]{2,1,0:T(8,128)(2,1)S(1)}) custom-call(s32[2]{0:T(128)S(1)} %copy-done.6, bf16[256,1024]{1,0:T(8,128)(2,1)S(1)} %bitcast.17, bf16[256,1024]{1,0:T(8,128)(2,1)S(1)} %bitcast.20, ...), custom_call_target="tpu_custom_call" | custom-call | flops 1000000000 | bytes 8388608 | tf_op jit(solution)/shard_map/time_second/pallas_call | solution.py:337
  45.1 0.0 collective-permute-done.5.g1
  45.1 0.7 collective-permute-done.6.g2
  45.8 1.3 %collective-permute-done.7.g3 = bf16[64,1024]{1,0:T(8,128)(2,1)S(1)} collective-permute-done((bf16[64,1024]{1,0:T(8,128)(2,1)S(1)}, bf16[64,1024]{1,0:T(8,128)(2,1)S(1)}, u32[]{:S(2)}, u32[]{:S(2)}) %collective-permute-start.7) | collective-permute-done | bytes 131104 | tf_op jit(solution)/shard_map/ppermute | solution.py:522
  47.2 0.0 copy-done.8
  47.2 6.2 %back_sides.1 = (bf16[2,256,1024]{2,1,0:T(8,128)(2,1)S(1)}, bf16[2,256,1024]{2,1,0:T(8,128)(2,1)S(1)}, f32[1024,256]{1,0:T(8,128)S(1)}) custom-call(s32[2]{0:T(128)S(1)} %copy-done.6, s32[8]{0:T(128)S(1)} %reshape_squeeze.3.lists, bf16[256,1024]{1,0:T(8,128)(2,1)S(1)} %bitcast.32, bf16[2,256,1024]{2,1,0:T(8,128)(2,1)S(1)} %collective-permute-done.low.from_low, ...), custom_call_target="tpu_custom_call" | custom-call | flops 6000000000 | bytes 16777216 | tf_op jit(solution)/shard_map/back_sides/pallas_call | solution.py:406
  53.4 2.9 %collective-permute-start.11 = (bf16[2,256,1024]{2,1,0:T(8,128)(2,1)S(1)}, bf16[2,256,1024]{2,1,0:T(8,128)(2,1)S(1)}, u32[]{:S(2)}, u32[]{:S(2)}) collective-permute-start(bf16[2,256,1024]{2,1,0:T(8,128)(2,1)S(1)} %get-tuple-element.60), channel_id=1, source_target_pairs={{0,4},{4,8},{8,12},{12,16},{16,20},{20,24},{24,28},{28,32},{32,36}... | collective-permute-start | bytes 3145736 | tf_op jit(solution)/shard_map/ppermute | solution.py:545
  56.3 0.0 collective-permute-start.12
  56.3 0.3 collective-permute-start.13
  56.6 1.3 %collective-permute-start.14 = (bf16[2,64,1024]{2,1,0:T(8,128)(2,1)S(1)}, bf16[2,64,1024]{2,1,0:T(8,128)(2,1)S(1)}, u32[]{:S(2)}, u32[]{:S(2)}) collective-permute-start(bf16[2,64,1024]{2,1,0:T(8,128)(2,1)S(1)} %get-tuple-element.65), channel_id=1, source_target_pairs={{0,2},{1,3},{2,0},{3,1},{4,6},{5,7},{6,4},{7,5},{8,10},{9,11},{10,... | collective-permute-start | bytes 786440 | tf_op jit(solution)/shard_map/ppermute | solution.py:522
  57.9 0.6 collective-permute-start.15
  58.5 4.9 %back_own.1 = (bf16[256,1024]{1,0:T(8,128)(2,1)}, f32[2,256,1024]{2,1,0:T(8,128)S(1)}) custom-call(s32[2]{0:T(128)S(1)} %copy-done.6, bf16[256,1024]{1,0:T(8,128)(2,1)S(1)} %bitcast.33, bf16[256,1024]{1,0:T(8,128)(2,1)S(1)} %bitcast.26, bf16[256,1024]{1,0:T(8,128)(2,1)S(1)} %bitcast.29, bf16[8,256,512]{2,1,0:T(8,128)(2,1)S(1)} %get-tuple-element.37.weights, ...), custom_call_target="tpu_custom_call" | custom-call | flops 6000000000 | bytes 16777216 | tf_op jit(solution)/shard_map/back_own/pallas_call | solution.py:456
  63.3 1.3 %collective-permute-done.13.t1 = bf16[2,64,1024]{2,1,0:T(8,128)(2,1)S(1)} collective-permute-done((bf16[2,64,1024]{2,1,0:T(8,128)(2,1)S(1)}, bf16[2,64,1024]{2,1,0:T(8,128)(2,1)S(1)}, u32[]{:S(2)}, u32[]{:S(2)}) %collective-permute-start.13) | collective-permute-done | bytes 262176 | tf_op jit(solution)/shard_map/ppermute | solution.py:522
  64.7 1.5 %collective-permute-done.14.t2 = bf16[2,64,1024]{2,1,0:T(8,128)(2,1)S(1)} collective-permute-done((bf16[2,64,1024]{2,1,0:T(8,128)(2,1)S(1)}, bf16[2,64,1024]{2,1,0:T(8,128)(2,1)S(1)}, u32[]{:S(2)}, u32[]{:S(2)}) %collective-permute-start.14) | collective-permute-done | bytes 262176 | tf_op jit(solution)/shard_map/ppermute | solution.py:522
  66.2 4.6 %collective-permute-done.15.t3 = bf16[2,64,1024]{2,1,0:T(8,128)(2,1)S(1)} collective-permute-done((bf16[2,64,1024]{2,1,0:T(8,128)(2,1)S(1)}, bf16[2,64,1024]{2,1,0:T(8,128)(2,1)S(1)}, u32[]{:S(2)}, u32[]{:S(2)}) %collective-permute-start.15) | collective-permute-done | bytes 262176 | tf_op jit(solution)/shard_map/ppermute | solution.py:522
  70.8 1.6 %finish_time.1 = (bf16[256,1024]{1,0:T(8,128)(2,1)}, bf16[256,1024]{1,0:T(8,128)(2,1)}) custom-call(s32[2]{0:T(128)S(1)} %copy-done.6, bf16[2,64,1024]{2,1,0:T(8,128)(2,1)S(1)} %get-tuple-element.56.after.t0, bf16[2,64,1024]{2,1,0:T(8,128)(2,1)S(1)} %collective-permute-done.13.t1, bf16[2,64,1024]{2,1,0:T(8,128)(2,1)S(1)} %collective-permute-done.14.t2, ...), custom_call_target="tpu_custom_call" | custom-call | bytes 2097152 | tf_op jit(solution)/shard_map/finish_time/pallas_call | solution.py:479
  72.3 0.0 collective-permute-done.11.low
  72.4 0.0 collective-permute-done.12.high
  72.4 1.2 %finish.1 = (bf16[256,1024]{1,0:T(8,128)(2,1)}, bf16[256,1024]{1,0:T(8,128)(2,1)}) custom-call(f32[2,256,1024]{2,1,0:T(8,128)S(1)} %get-tuple-element.59.totals, bf16[2,256,1024]{2,1,0:T(8,128)(2,1)S(1)} %collective-permute-done.11.low, bf16[2,256,1024]{2,1,0:T(8,128)(2,1)S(1)} %collective-permute-done.12.high), custom_call_target="tpu_custom_call" | custom-call | bytes 5242880 | tf_op jit(solution)/shard_map/finish/pallas_call | solution.py:496
  (4 shorter events, 0.0 us)
Async XLA Ops:
  0.6 11.4 %copy-start = (s32[64,2,4,2]{0,3,2,1:T(2,128)S(1)}, s32[64,2,4,2]{0,3,2,1:T(2,128)}, u32[]{:S(2)}) copy-start(s32[64,2,4,2]{0,3,2,1:T(2,128)} %param.17) | copy-start | bytes 12292
  0.6 11.7 %copy-start.4 = (bf16[1,256,1024]{2,1,0:T(8,128)(2,1)S(1)}, bf16[1,256,1024]{2,1,0:T(8,128)(2,1)}, u32[]{:S(2)}) copy-start(bf16[1,256,1024]{2,1,0:T(8,128)(2,1)} %param.10) | copy-start | bytes 1572868
  0.7 11.7 %copy-start.5 = (bf16[1,256,1024]{2,1,0:T(8,128)(2,1)S(1)}, bf16[1,256,1024]{2,1,0:T(8,128)(2,1)}, u32[]{:S(2)}) copy-start(bf16[1,256,1024]{2,1,0:T(8,128)(2,1)} %param.11) | copy-start | bytes 1572868
  0.7 11.7 %copy-start.10 = (s32[128]{0:T(128)S(1)}, s32[128]{0:T(128)}, u32[]{:S(2)}) copy-start(s32[128]{0:T(128)} %fluid.3) | copy-start | bytes 1540
  0.7 11.7 %copy-start.9 = (s32[16384]{0:T(1024)S(1)}, s32[16384]{0:T(1024)}, u32[]{:S(2)}) copy-start(s32[16384]{0:T(1024)} %param.16) | copy-start | bytes 196612
  1.3 11.1 %copy-start.6 = (s32[2]{0:T(128)S(1)}, s32[2]{0:T(128)}, u32[]{:S(2)}) copy-start(s32[2]{0:T(128)} %pad_add_fusion.place) | copy-start | bytes 28
  4.8 15.5 %collective-permute-start = (bf16[2,256,1024]{2,1,0:T(8,128)(2,1)}, bf16[2,256,1024]{2,1,0:T(8,128)(2,1)S(1)}, u32[]{:S(2)}, u32[]{:S(2)}) collective-permute-start(bf16[2,256,1024]{2,1,0:T(8,128)(2,1)} %get-tuple-element.38), channel_id=1, source_target_pairs={{0,4},{4,8},{8,12},{12,16},{16,20},{20,24},{24,28},{28,32},{32,36}... | collective-permute-start | bytes 3145736 | tf_op jit(solution)/shard_map/ppermute | solution.py:528
  8.3 15.9 %collective-permute-start.1 = (bf16[2,256,1024]{2,1,0:T(8,128)(2,1)}, bf16[2,256,1024]{2,1,0:T(8,128)(2,1)}, u32[]{:S(2)}, u32[]{:S(2)}) collective-permute-start(bf16[2,256,1024]{2,1,0:T(8,128)(2,1)} %get-tuple-element.38), channel_id=1, source_target_pairs={{0,252},{4,0},{8,4},{12,8},{16,12},{20,16},{24,20},{28,24},{32,28}... | collective-permute-start | bytes 3145736 | tf_op jit(solution)/shard_map/ppermute | solution.py:528
  8.3 25.6 %collective-permute-start.2 = (bf16[3,64,1024]{2,1,0:T(8,128)(2,1)}, bf16[3,64,1024]{2,1,0:T(8,128)(2,1)S(1)}, u32[]{:S(2)}, u32[]{:S(2)}) collective-permute-start(bf16[3,64,1024]{2,1,0:T(8,128)(2,1)} %get-tuple-element.44), channel_id=1, source_target_pairs={{0,3},{1,0},{2,1},{3,2},{4,7},{5,4},{6,5},{7,6},{8,11},{9,8},{10,9... | collective-permute-start | bytes 1179656 | tf_op jit(solution)/shard_map/ppermute | solution.py:522
  11.0 23.5 %collective-permute-start.3 = (bf16[3,64,1024]{2,1,0:T(8,128)(2,1)}, bf16[3,64,1024]{2,1,0:T(8,128)(2,1)S(1)}, u32[]{:S(2)}, u32[]{:S(2)}) collective-permute-start(bf16[3,64,1024]{2,1,0:T(8,128)(2,1)} %get-tuple-element.45), channel_id=1, source_target_pairs={{0,2},{1,3},{2,0},{3,1},{4,6},{5,7},{6,4},{7,5},{8,10},{9,11},{10,... | collective-permute-start | bytes 1179656 | tf_op jit(solution)/shard_map/ppermute | solution.py:522
  11.3 23.2 %collective-permute-start.4 = (bf16[3,64,1024]{2,1,0:T(8,128)(2,1)}, bf16[3,64,1024]{2,1,0:T(8,128)(2,1)S(1)}, u32[]{:S(2)}, u32[]{:S(2)}) collective-permute-start(bf16[3,64,1024]{2,1,0:T(8,128)(2,1)} %get-tuple-element.46), channel_id=1, source_target_pairs={{0,1},{1,2},{2,3},{3,0},{4,5},{5,6},{6,7},{7,4},{8,9},{9,10},{10,1... | collective-permute-start | bytes 1179656 | tf_op jit(solution)/shard_map/ppermute | solution.py:522
  12.4 1.0 %copy-start.7 = (bf16[1,256,1024]{2,1,0:T(8,128)(2,1)S(1)}, bf16[1,256,1024]{2,1,0:T(8,128)(2,1)}, u32[]{:S(2)}) copy-start(bf16[1,256,1024]{2,1,0:T(8,128)(2,1)} %param.9) | copy-start | bytes 1572868
  24.2 10.3 %copy-start.1 = (bf16[1,256,1024]{2,1,0:T(8,128)(2,1)S(1)}, bf16[1,256,1024]{2,1,0:T(8,128)(2,1)}, u32[]{:S(2)}) copy-start(bf16[1,256,1024]{2,1,0:T(8,128)(2,1)} %param.12) | copy-start | bytes 1572868
  24.2 10.3 %copy-start.2 = (bf16[1,256,1024]{2,1,0:T(8,128)(2,1)S(1)}, bf16[1,256,1024]{2,1,0:T(8,128)(2,1)}, u32[]{:S(2)}) copy-start(bf16[1,256,1024]{2,1,0:T(8,128)(2,1)} %param.13) | copy-start | bytes 1572868
  24.2 10.3 %copy-start.3 = (bf16[1,256,1024]{2,1,0:T(8,128)(2,1)S(1)}, bf16[1,256,1024]{2,1,0:T(8,128)(2,1)}, u32[]{:S(2)}) copy-start(bf16[1,256,1024]{2,1,0:T(8,128)(2,1)} %param.14) | copy-start | bytes 1572868
  30.8 10.8 %collective-permute-start.8 = (bf16[64,1024]{1,0:T(8,128)(2,1)S(1)}, bf16[64,1024]{1,0:T(8,128)(2,1)S(1)}, u32[]{:S(2)}, u32[]{:S(2)}) collective-permute-start(bf16[64,1024]{1,0:T(8,128)(2,1)S(1)} %get-tuple-element.53), channel_id=1, source_target_pairs={{0,3},{1,0},{2,1},{3,2},{4,7},{5,4},{6,5},{7,6},{8,11},{9,8},{10,9... | collective-permute-start | bytes 393224 | tf_op jit(solution)/shard_map/ppermute | solution.py:522
  33.6 8.0 %collective-permute-start.9 = (bf16[64,1024]{1,0:T(8,128)(2,1)S(1)}, bf16[64,1024]{1,0:T(8,128)(2,1)S(1)}, u32[]{:S(2)}, u32[]{:S(2)}) collective-permute-start(bf16[64,1024]{1,0:T(8,128)(2,1)S(1)} %get-tuple-element.54), channel_id=1, source_target_pairs={{0,2},{1,3},{2,0},{3,1},{4,6},{5,7},{6,4},{7,5},{8,10},{9,11},{10,... | collective-permute-start | bytes 393224 | tf_op jit(solution)/shard_map/ppermute | solution.py:522
  33.9 7.8 %collective-permute-start.10 = (bf16[64,1024]{1,0:T(8,128)(2,1)S(1)}, bf16[64,1024]{1,0:T(8,128)(2,1)S(1)}, u32[]{:S(2)}, u32[]{:S(2)}) collective-permute-start(bf16[64,1024]{1,0:T(8,128)(2,1)S(1)} %get-tuple-element.55), channel_id=1, source_target_pairs={{0,1},{1,2},{2,3},{3,0},{4,5},{5,6},{6,7},{7,4},{8,9},{9,10},{10,1... | collective-permute-start | bytes 393224 | tf_op jit(solution)/shard_map/ppermute | solution.py:522
  38.0 7.2 %collective-permute-start.5 = (bf16[64,1024]{1,0:T(8,128)(2,1)S(1)}, bf16[64,1024]{1,0:T(8,128)(2,1)S(1)}, u32[]{:S(2)}, u32[]{:S(2)}) collective-permute-start(bf16[64,1024]{1,0:T(8,128)(2,1)S(1)} %get-tuple-element.49), channel_id=1, source_target_pairs={{0,3},{1,0},{2,1},{3,2},{4,7},{5,4},{6,5},{7,6},{8,11},{9,8},{10,9... | collective-permute-start | bytes 393224 | tf_op jit(solution)/shard_map/ppermute | solution.py:522
  40.1 5.7 %collective-permute-start.6 = (bf16[64,1024]{1,0:T(8,128)(2,1)S(1)}, bf16[64,1024]{1,0:T(8,128)(2,1)S(1)}, u32[]{:S(2)}, u32[]{:S(2)}) collective-permute-start(bf16[64,1024]{1,0:T(8,128)(2,1)S(1)} %get-tuple-element.50), channel_id=1, source_target_pairs={{0,2},{1,3},{2,0},{3,1},{4,6},{5,7},{6,4},{7,5},{8,10},{9,11},{10,... | collective-permute-start | bytes 393224 | tf_op jit(solution)/shard_map/ppermute | solution.py:522
  41.7 5.5 %collective-permute-start.7 = (bf16[64,1024]{1,0:T(8,128)(2,1)S(1)}, bf16[64,1024]{1,0:T(8,128)(2,1)S(1)}, u32[]{:S(2)}, u32[]{:S(2)}) collective-permute-start(bf16[64,1024]{1,0:T(8,128)(2,1)S(1)} %get-tuple-element.51), channel_id=1, source_target_pairs={{0,1},{1,2},{2,3},{3,0},{4,5},{5,6},{6,7},{7,4},{8,9},{9,10},{10,1... | collective-permute-start | bytes 393224 | tf_op jit(solution)/shard_map/ppermute | solution.py:522
  41.7 5.5 %copy-start.8 = (bf16[1,256,1024]{2,1,0:T(8,128)(2,1)S(1)}, bf16[1,256,1024]{2,1,0:T(8,128)(2,1)}, u32[]{:S(2)}) copy-start(bf16[1,256,1024]{2,1,0:T(8,128)(2,1)} %param.9) | copy-start | bytes 1572868
  53.4 18.9 %collective-permute-start.11 = (bf16[2,256,1024]{2,1,0:T(8,128)(2,1)S(1)}, bf16[2,256,1024]{2,1,0:T(8,128)(2,1)S(1)}, u32[]{:S(2)}, u32[]{:S(2)}) collective-permute-start(bf16[2,256,1024]{2,1,0:T(8,128)(2,1)S(1)} %get-tuple-element.60), channel_id=1, source_target_pairs={{0,4},{4,8},{8,12},{12,16},{16,20},{20,24},{24,28},{28,32},{32,36}... | collective-permute-start | bytes 3145736 | tf_op jit(solution)/shard_map/ppermute | solution.py:545
  56.3 16.1 %collective-permute-start.12 = (bf16[2,256,1024]{2,1,0:T(8,128)(2,1)S(1)}, bf16[2,256,1024]{2,1,0:T(8,128)(2,1)S(1)}, u32[]{:S(2)}, u32[]{:S(2)}) collective-permute-start(bf16[2,256,1024]{2,1,0:T(8,128)(2,1)S(1)} %get-tuple-element.61), channel_id=1, source_target_pairs={{0,252},{4,0},{8,4},{12,8},{16,12},{20,16},{24,20},{28,24},{32,28}... | collective-permute-start | bytes 3145736 | tf_op jit(solution)/shard_map/ppermute | solution.py:544
  56.3 8.4 %collective-permute-start.13 = (bf16[2,64,1024]{2,1,0:T(8,128)(2,1)S(1)}, bf16[2,64,1024]{2,1,0:T(8,128)(2,1)S(1)}, u32[]{:S(2)}, u32[]{:S(2)}) collective-permute-start(bf16[2,64,1024]{2,1,0:T(8,128)(2,1)S(1)} %get-tuple-element.64), channel_id=1, source_target_pairs={{0,3},{1,0},{2,1},{3,2},{4,7},{5,4},{6,5},{7,6},{8,11},{9,8},{10,9... | collective-permute-start | bytes 786440 | tf_op jit(solution)/shard_map/ppermute | solution.py:522
  56.6 9.6 %collective-permute-start.14 = (bf16[2,64,1024]{2,1,0:T(8,128)(2,1)S(1)}, bf16[2,64,1024]{2,1,0:T(8,128)(2,1)S(1)}, u32[]{:S(2)}, u32[]{:S(2)}) collective-permute-start(bf16[2,64,1024]{2,1,0:T(8,128)(2,1)S(1)} %get-tuple-element.65), channel_id=1, source_target_pairs={{0,2},{1,3},{2,0},{3,1},{4,6},{5,7},{6,4},{7,5},{8,10},{9,11},{10,... | collective-permute-start | bytes 786440 | tf_op jit(solution)/shard_map/ppermute | solution.py:522
  57.9 12.9 %collective-permute-start.15 = (bf16[2,64,1024]{2,1,0:T(8,128)(2,1)S(1)}, bf16[2,64,1024]{2,1,0:T(8,128)(2,1)S(1)}, u32[]{:S(2)}, u32[]{:S(2)}) collective-permute-start(bf16[2,64,1024]{2,1,0:T(8,128)(2,1)S(1)} %get-tuple-element.66), channel_id=1, source_target_pairs={{0,1},{1,2},{2,3},{3,0},{4,5},{5,6},{6,7},{7,4},{8,9},{9,10},{10,1... | collective-permute-start | bytes 786440 | tf_op jit(solution)/shard_map/ppermute | solution.py:522

commit v2 on v1

--- a/solution.py
+++ b/solution.py
@@ -27,6 +27,10 @@
 
 def dot(a, b):
     return jnp.dot(a, b, preferred_element_type=F32)
+
+
+def dot_t(a, b):
+    return lax.dot_general(a, b, (((1,), (1,)), ((), ())), preferred_element_type=F32)
 
 
 def kernel_params(mib):
@@ -363,7 +367,7 @@
 
 def back_sides_kernel(
     place, lists, q, from_low, from_high, probs, states_t, g0, g1, g2, g3, after,
-    to_low, to_high, query_part, sg,
+    to_low, to_high, slopes, sg,
 ):
     low_ids, high_ids = listed(place, lists, 0), listed(place, lists, 1)
     grad_rows(sg, place, (g0, g1, g2, g3))
@@ -373,22 +377,19 @@
         rows = pl.ds(pl.multiple_of(p * 128, 128), 128)
         sg_p = sg[:, lanes]
         sg_t = transposed(sg_p)
-        sg_cols, sg_rows, q_rows = grouped_lanes(sg_t), grouped_rows(sg_p), grouped_rows(q[:, lanes])
+        sg_cols = grouped_lanes(sg_t)
+        q_cols = grouped_lanes((q[:, lanes].astype(F32) * SCALE).T.astype(BF16))
         delta = deltas(sg_t, states_t[rows, :])
         key_parts, value_parts = [], []
         for b in range(2):
             cols = slice(256 * b, 256 * b + 256)
-            k_n = neighbour_rows(from_low.at[0], from_high.at[0], low_ids, high_ids, b, lanes)
             v_n = neighbour_rows(from_low.at[1], from_high.at[1], low_ids, high_ids, b, lanes)
-            k_n_t = transposed(k_n)
             dp = dot(v_n, sg_cols[:, cols])
             pr = probs[p, :, cols]
             ds = (pr.astype(F32) * (dp - delta[:, cols])).astype(BF16)
-            query_part[rows, b * 128 : b * 128 + 128] = jnp.concatenate(
-                [dot(k_n_t[:HD], ds[:, :BLOCK]), dot(k_n_t[HD:], ds[:, BLOCK:])], axis=0
-            )
-            key_parts.append(dot(ds, q_rows[cols]) * SCALE)
-            value_parts.append(dot(pr, sg_rows[cols]))
+            slopes[p, :, cols] = ds
+            key_parts.append(dot_t(q_cols[:, cols], ds).T)
+            value_parts.append(dot_t(sg_cols[:, cols], pr).T)
         for n, parts in enumerate((key_parts, value_parts)):
             for ids, out, side in ((low_ids, to_low, 0), (high_ids, to_high, 1)):
                 for j in range(2):
@@ -407,7 +408,7 @@
         back_sides_kernel,
         in_specs=[SMEM_SPEC] * 2 + [VMEM_SPEC] * 9 + [ANY_SPEC],
         out_specs=[VMEM_SPEC] * 3,
-        out_shape=[message, message, jax.ShapeDtypeStruct((D, TOK), F32)],
+        out_shape=[message, message, jax.ShapeDtypeStruct((PAIRS, TOK, 512), BF16)],
         scratch_shapes=[pltpu.VMEM((TOK, D), BF16)],
         compiler_params=kernel_params(32),
         cost_estimate=cost(6_000_000_000, 16 << 20),
@@ -416,8 +417,10 @@
 
 
 def back_own_kernel(
-    place, q, k, v, weights, factors, states_t, query_part, g0, g1, g2, g3, query_grad, totals, sg
+    place, lists, q, k, v, from_high, from_low, weights, factors, states_t, slopes, g0, g1, g2, g3,
+    query_grad, totals, sg,
 ):
+    low_ids, high_ids = listed(place, lists, 0), listed(place, lists, 1)
     grad_rows(sg, place, (g0, g1, g2, g3))
 
     def pair(p):
@@ -434,17 +437,17 @@
         dp = dot(v[:, lanes], sg_cols)
         pr = weights[p]
         ds = (pr.astype(F32) * (dp - delta)).astype(BF16)
-        cols = [
-            jnp.concatenate(
-                [
-                    dot(k_t[:HD], ds[:, 256 * b : 256 * b + 128]),
-                    dot(k_t[HD:], ds[:, 256 * b + 128 : 256 * b + 256]),
-                ],
-                axis=0,
+        blocks = []
+        for b in range(2):
+            k_n_t = transposed(
+                neighbour_rows(from_low.at[0], from_high.at[0], low_ids, high_ids, b, lanes)
             )
-            for b in range(2)
-        ]
-        query_t = jnp.concatenate(cols, axis=1) + query_part[rows, :]
+            for h in range(2):
+                half, cols = slice(h * HD, h * HD + HD), slice(256 * b + 128 * h, 256 * b + 128 * h + 128)
+                blocks.append(dot(k_t[half], ds[:, cols]) + dot(k_n_t[half], slopes[p, :, cols]))
+        query_t = jnp.concatenate(
+            [jnp.concatenate(blocks[:2], axis=0), jnp.concatenate(blocks[2:], axis=0)], axis=1
+        )
         query_grad[:, lanes] = (query_t * SCALE).T.astype(BF16)
         totals[0, :, lanes] = dot(ds, q_rows) * SCALE
         totals[1, :, lanes] = dot(pr, sg_rows)
@@ -452,10 +455,10 @@
     pl.loop(0, PAIRS, unroll=8)(pair)
 
 
-def back_own(place, q, k, v, weights, factors, states_t, query_part, pieces):
+def back_own(place, lists, q, k, v, low, high, weights, factors, states_t, slopes, pieces):
     return pl.pallas_call(
         back_own_kernel,
-        in_specs=[SMEM_SPEC] + [VMEM_SPEC] * 11,
+        in_specs=[SMEM_SPEC] * 2 + [VMEM_SPEC] * 13,
         out_specs=[VMEM_SPEC] * 2,
         out_shape=[
             jax.ShapeDtypeStruct((TOK, D), BF16),
@@ -465,7 +468,7 @@
         compiler_params=kernel_params(32),
         cost_estimate=cost(6_000_000_000, 16 << 20),
         name="back_own",
-    )(place, q, k, v, weights, factors, states_t, query_part, *pieces)
+    )(place, lists, q, k, v, high, low, weights, factors, states_t, slopes, *pieces)
 
 
 def finish_time_kernel(place, t0, t1, t2, t3, query_t, key_t):
@@ -538,17 +541,17 @@
     there = {(4 - d) % 4: shift(pieces[d], d) for d in (1, 3, 2)}
     back = time_second(place, qt, kt, og, *ms, attn, pieces[0], there[1], there[2], there[3])
 
-    to_low, to_high, query_part = back_sides(
+    to_low, to_high, slopes = back_sides(
         place, lists, q, low, high, probs, states_t, grad_pieces, back[0]
     )
     from_high = lax.ppermute(to_low, "space", down)
     from_low = lax.ppermute(to_high, "space", up)
     returned = {(4 - d) % 4: shift(back[d], d) for d in (1, 3, 2)}
+    query_grad, totals = back_own(
+        place, lists, q, k, v, low, high, weights, factors, states_t, slopes, grad_pieces
+    )
     query_time_grad, key_time_grad = finish_time(
         place, (back[0], returned[1], returned[2], returned[3])
-    )
-    query_grad, totals = back_own(
-        place, q, k, v, weights, factors, states_t, query_part, grad_pieces
     )
     key_grad, value_grad = finish(totals, from_low, from_high)
     return tuple(

time: 74.4 us -> 73.5 us (0.988)
  waiting for transfers between devices: 16.6 us -> 15.7 us
    pallas_call x1, Pallas kernels: 6.23 us -> 5.25 us  [back_sides(): pl.pallas_call(back_sides_kernel, in_specs=[SMEM_SPEC] * 2 + [VMEM_SPEC]...]
    ppermute x12, waiting for transfers between devices: 9.49 us -> 8.58 us  [shift(): return lax.ppermute(x, 'tm', [(i, (i + d) % steps) for i in range(steps)])]
    pallas_call x1, Pallas kernels: 4.88 us -> 5.76 us  [back_own(): pl.pallas_call(back_own_kernel, in_specs=[SMEM_SPEC] * 2 + [VMEM_SPEC] *...]
  transfers between devices with their start and end apart: 16 -> 16, of which waited for: 7 -> 7; matrix products, arithmetic and copies ran while one was open for 0% -> 0% of each run, Pallas kernels for 32% -> 34%
where the time goes in v2:
time: 73.5 us; the launch traced here: 72.6 us
  Pallas kernels  34.4 us (47%)
  starting transfers between devices  19.6 us (27%)
  waiting for transfers between devices  15.7 us (21%)
  local copies, waits for them, and re-layouts  1.38 us (2%)
  between operations  0.82 us (1%)
    ppermute x12, starting transfers between devices, shift(): return lax.ppermute(x, 'tm', [(i, (i + d) % steps) for i in range(steps)])  13.3 us
    ppermute x12, waiting for transfers between devices, shift(): return lax.ppermute(x, 'tm', [(i, (i + d) % steps) for i in range(steps)])  8.58 us
    ppermute x2, waiting for transfers between devices, body(): low, high = (lax.ppermute(kv, 'space', up), lax.ppermute(kv, 'space', down))  7.13 us
    pallas_call x1, Pallas kernels, forward_sides(): pl.pallas_call(forward_sides_kernel, in_specs=[SMEM_SPEC] * 3 + [VMEM_SPE...  6.62 us
    pallas_call x1, Pallas kernels, back_own(): pl.pallas_call(back_own_kernel, in_specs=[SMEM_SPEC] * 2 + [VMEM_SPEC] *...  5.76 us
    pallas_call x1, Pallas kernels, back_sides(): pl.pallas_call(back_sides_kernel, in_specs=[SMEM_SPEC] * 2 + [VMEM_SPEC]...  5.25 us
    pallas_call x1, Pallas kernels, forward_own(): pl.pallas_call(forward_own_kernel, in_specs=[SMEM_SPEC] * 2 + [VMEM_SPEC]...  3.64 us
    ppermute x2, starting transfers between devices, body(): low, high = (lax.ppermute(kv, 'space', up), lax.ppermute(kv, 'space', down))  3.49 us
  transfers between devices with their start and end apart: 16, of which 7 were waited for; matrix products, arithmetic and copies ran while one was open for 0% of the time, Pallas kernels for 34%

profile of v2, /device:TPU:103, one launch (start us, length us, event | category | flops | bytes accessed | tf_op | source)
XLA Modules:
  0.0 72.6 jit_solution(679683178381882496)
XLA Ops:
  0.6 0.0 copy-start
  0.6 0.0 copy-start.5
  0.7 0.0 copy-start.4
  0.7 0.0 copy-start.10
  0.7 0.0 copy-start.9
  0.7 0.6 pad_add_fusion.place
  1.3 0.0 copy-start.6
  1.3 3.5 %stage.1 = (bf16[3,64,1024]{2,1,0:T(8,128)(2,1)}, bf16[3,64,1024]{2,1,0:T(8,128)(2,1)}, bf16[3,64,1024]{2,1,0:T(8,128)(2,1)}, bf16[2,256,1024]{2,1,0:T(8,128)(2,1)}) custom-call(s32[2]{0:T(128)} %pad_add_fusion.place, bf16[256,1024]{1,0:T(8,128)(2,1)} %bitcast.15, bf16[256,1024]{1,0:T(8,128)(2,1)} %bitcast.18, bf16[256,1024]{1,0:T(8,128)(2,1)} %bitcast.21, ...), custom_call_target="tpu_custom_call" | custom-call | bytes 4194304 | tf_op jit(solution)/shard_map/stage/pallas_call | solution.py:92
  4.8 3.5 %collective-permute-start.1 = (bf16[2,256,1024]{2,1,0:T(8,128)(2,1)}, bf16[2,256,1024]{2,1,0:T(8,128)(2,1)S(1)}, u32[]{:S(2)}, u32[]{:S(2)}) collective-permute-start(bf16[2,256,1024]{2,1,0:T(8,128)(2,1)} %get-tuple-element.37), channel_id=1, source_target_pairs={{0,4},{4,8},{8,12},{12,16},{16,20},{20,24},{24,28},{28,32},{32,36}... | collective-permute-start | bytes 3145736 | tf_op jit(solution)/shard_map/ppermute | solution.py:531
  8.3 0.0 collective-permute-start
  8.3 2.7 %collective-permute-start.2 = (bf16[3,64,1024]{2,1,0:T(8,128)(2,1)}, bf16[3,64,1024]{2,1,0:T(8,128)(2,1)S(1)}, u32[]{:S(2)}, u32[]{:S(2)}) collective-permute-start(bf16[3,64,1024]{2,1,0:T(8,128)(2,1)} %get-tuple-element.44), channel_id=1, source_target_pairs={{0,3},{1,0},{2,1},{3,2},{4,7},{5,4},{6,5},{7,6},{8,11},{9,8},{10,9... | collective-permute-start | bytes 1179656 | tf_op jit(solution)/shard_map/ppermute | solution.py:525
  11.0 0.3 collective-permute-start.3
  11.3 0.7 collective-permute-start.4
  12.0 0.0 copy-done
  12.0 0.1 constant_dynamic-slice_fusion
  12.1 0.1 copy.14
  12.2 0.1 reshape_squeeze.3.lists
  12.3 0.0 copy-done.5
  12.3 0.0 copy-done.4
  12.3 0.0 copy-done.10
  12.3 0.0 copy-done.9
  12.4 0.0 copy-done.6
  12.4 0.0 copy-start.7
  12.4 1.0 %copy-done.7 = bf16[1,256,1024]{2,1,0:T(8,128)(2,1)S(1)} copy-done((bf16[1,256,1024]{2,1,0:T(8,128)(2,1)S(1)}, bf16[1,256,1024]{2,1,0:T(8,128)(2,1)}, u32[]{:S(2)}) %copy-start.7) | copy-done | bytes 524312
  13.4 0.0 copy-start.8
  13.4 3.6 %forward_own.1 = (bf16[8,256,512]{2,1,0:T(8,128)(2,1)S(1)}, f32[8,8,512]{2,1,0:T(8,128)S(1)}, f32[1024,256]{1,0:T(8,128)S(1)}) custom-call(s32[2]{0:T(128)S(1)} %copy-done.6, s32[128]{0:T(128)S(1)} %copy-done.10, s32[128,128]{1,0:T(8,128)S(1)} %bitcast.34, bf16[256,1024]{1,0:T(8,128)(2,1)S(1)} %bitcast.30, bf16[256,1024]{1,0:T(8,128)(2,1)S(1)} %bitcast.25, ...), custom_call_target="tpu_custom_call" | custom-call | flops 2000000000 | bytes 8388608 | tf_op jit(solution)/shard_map/forward_own/pallas_call | solution.py:160
  17.1 3.3 %collective-permute-done.1.low.from_low = bf16[2,256,1024]{2,1,0:T(8,128)(2,1)S(1)} collective-permute-done((bf16[2,256,1024]{2,1,0:T(8,128)(2,1)}, bf16[2,256,1024]{2,1,0:T(8,128)(2,1)S(1)}, u32[]{:S(2)}, u32[]{:S(2)}) %collective-permute-start.1) | collective-permute-done | bytes 1048608 | tf_op jit(solution)/shard_map/ppermute | solution.py:531
  20.3 3.9 %collective-permute-done.high.from_high = bf16[2,256,1024]{2,1,0:T(8,128)(2,1)} collective-permute-done((bf16[2,256,1024]{2,1,0:T(8,128)(2,1)}, bf16[2,256,1024]{2,1,0:T(8,128)(2,1)}, u32[]{:S(2)}, u32[]{:S(2)}) %collective-permute-start) | collective-permute-done | bytes 1048608 | tf_op jit(solution)/shard_map/ppermute | solution.py:531
  24.2 0.0 copy-done.8
  24.2 6.6 %forward_sides.1 = (bf16[64,1024]{1,0:T(8,128)(2,1)S(1)}, bf16[64,1024]{1,0:T(8,128)(2,1)S(1)}, bf16[64,1024]{1,0:T(8,128)(2,1)S(1)}, bf16[64,1024]{1,0:T(8,128)...) custom-call(s32[2]{0:T(128)S(1)} %copy-done.6, ...), custom_call_target="tpu_custom_call" | custom-call | flops 2000000000 | bytes 8388608 | tf_op jit(solution)/shard_map/forward_sides/pallas_call | solution.py:230
  30.8 2.8 %collective-permute-start.8 = (bf16[64,1024]{1,0:T(8,128)(2,1)S(1)}, bf16[64,1024]{1,0:T(8,128)(2,1)S(1)}, u32[]{:S(2)}, u32[]{:S(2)}) collective-permute-start(bf16[64,1024]{1,0:T(8,128)(2,1)S(1)} %get-tuple-element.53), channel_id=1, source_target_pairs={{0,3},{1,0},{2,1},{3,2},{4,7},{5,4},{6,5},{7,6},{8,11},{9,8},{10,9... | collective-permute-start | bytes 393224 | tf_op jit(solution)/shard_map/ppermute | solution.py:525
  33.6 0.3 collective-permute-start.9
  33.9 0.0 collective-permute-done.2.m1
  33.9 0.6 collective-permute-start.10
  34.5 0.0 collective-permute-done.3.m2
  34.5 0.0 collective-permute-done.4.m3
  34.5 0.0 copy-done.1
  34.5 0.0 copy-done.2
  34.5 0.0 copy-done.3
  34.5 3.5 %time_first.1 = (bf16[64,1024]{1,0:T(8,128)(2,1)S(1)}, bf16[64,1024]{1,0:T(8,128)(2,1)S(1)}, bf16[64,1024]{1,0:T(8,128)(2,1)S(1)}, bf16[64,1024]{1,0:T(8,128)(2,1)S(1)}, bf16[16,64,1024]{2,1,0:T(8,128)(2,1)S(1)}) custom-call(s32[2]{0:T(128)S(1)} %copy-done.6, bf16[256,1024]{1,0:T(8,128)(2,1)S(1)} %bitcast.16, bf16[256,1024]{1,0:T(8,128)(2,1)S(1)} %bitcast.19, ...), custom_call_target="tpu_custom_call" | custom-call | flops 1000000000 | bytes 8388608 | tf_op jit(solution)/shard_map/time_first/pallas_call | solution.py:295
  38.0 2.2 %collective-permute-start.5 = (bf16[64,1024]{1,0:T(8,128)(2,1)S(1)}, bf16[64,1024]{1,0:T(8,128)(2,1)S(1)}, u32[]{:S(2)}, u32[]{:S(2)}) collective-permute-start(bf16[64,1024]{1,0:T(8,128)(2,1)S(1)} %get-tuple-element.49), channel_id=1, source_target_pairs={{0,3},{1,0},{2,1},{3,2},{4,7},{5,4},{6,5},{7,6},{8,11},{9,8},{10,9... | collective-permute-start | bytes 393224 | tf_op jit(solution)/shard_map/ppermute | solution.py:525
  40.2 1.5 %collective-permute-start.6 = (bf16[64,1024]{1,0:T(8,128)(2,1)S(1)}, bf16[64,1024]{1,0:T(8,128)(2,1)S(1)}, u32[]{:S(2)}, u32[]{:S(2)}) collective-permute-start(bf16[64,1024]{1,0:T(8,128)(2,1)S(1)} %get-tuple-element.50), channel_id=1, source_target_pairs={{0,2},{1,3},{2,0},{3,1},{4,6},{5,7},{6,4},{7,5},{8,10},{9,11},{10,... | collective-permute-start | bytes 393224 | tf_op jit(solution)/shard_map/ppermute | solution.py:525
  41.7 0.0 collective-permute-done.8.x1
  41.7 0.0 collective-permute-start.7
  41.7 0.0 collective-permute-done.9.x2
  41.7 0.0 collective-permute-done.10.x3
  41.7 3.5 %time_second.1 = (bf16[2,64,1024]{2,1,0:T(8,128)(2,1)S(1)}, bf16[2,64,1024]{2,1,0:T(8,128)(2,1)S(1)}, bf16[2,64,1024]{2,1,0:T(8,128)(2,1)S(1)}, bf16[2,64,1024]{2,1,0:T(8,128)(2,1)S(1)}) custom-call(s32[2]{0:T(128)S(1)} %copy-done.6, bf16[256,1024]{1,0:T(8,128)(2,1)S(1)} %bitcast.17, bf16[256,1024]{1,0:T(8,128)(2,1)S(1)} %bitcast.20, ...), custom_call_target="tpu_custom_call" | custom-call | flops 1000000000 | bytes 8388608 | tf_op jit(solution)/shard_map/time_second/pallas_call | solution.py:341
  45.2 0.0 collective-permute-done.5.g1
  45.2 0.7 collective-permute-done.6.g2
  45.8 1.4 %collective-permute-done.7.g3 = bf16[64,1024]{1,0:T(8,128)(2,1)S(1)} collective-permute-done((bf16[64,1024]{1,0:T(8,128)(2,1)S(1)}, bf16[64,1024]{1,0:T(8,128)(2,1)S(1)}, u32[]{:S(2)}, u32[]{:S(2)}) %collective-permute-start.7) | collective-permute-done | bytes 131104 | tf_op jit(solution)/shard_map/ppermute | solution.py:525
  47.2 5.2 %back_sides.1 = (bf16[2,256,1024]{2,1,0:T(8,128)(2,1)S(1)}, bf16[2,256,1024]{2,1,0:T(8,128)(2,1)S(1)}, bf16[8,256,512]{2,1,0:T(8,128)(2,1)S(1)}) custom-call(s32[2]{0:T(128)S(1)} %copy-done.6, s32[8]{0:T(128)S(1)} %reshape_squeeze.3.lists, bf16[256,1024]{1,0:T(8,128)(2,1)S(1)} %bitcast.32, bf16[2,256,1024]{2,1,0:T(8,128)(2,1)S(1)} %collective-permute-done.1.low.from_low, ...), custom_call_target="tpu_custom_call" | custom-call | flops 6000000000 | bytes 16777216 | tf_op jit(solution)/shard_map/back_sides/pallas_call | solution.py:407
  52.4 2.9 %collective-permute-start.11 = (bf16[2,256,1024]{2,1,0:T(8,128)(2,1)S(1)}, bf16[2,256,1024]{2,1,0:T(8,128)(2,1)S(1)}, u32[]{:S(2)}, u32[]{:S(2)}) collective-permute-start(bf16[2,256,1024]{2,1,0:T(8,128)(2,1)S(1)} %get-tuple-element.60), channel_id=1, source_target_pairs={{0,4},{4,8},{8,12},{12,16},{16,20},{20,24},{24,28},{28,32},{32,36}... | collective-permute-start | bytes 3145736 | tf_op jit(solution)/shard_map/ppermute | solution.py:548
  55.3 0.0 collective-permute-start.12
  55.3 0.3 collective-permute-start.13
  55.6 1.3 %collective-permute-start.14 = (bf16[2,64,1024]{2,1,0:T(8,128)(2,1)S(1)}, bf16[2,64,1024]{2,1,0:T(8,128)(2,1)S(1)}, u32[]{:S(2)}, u32[]{:S(2)}) collective-permute-start(bf16[2,64,1024]{2,1,0:T(8,128)(2,1)S(1)} %get-tuple-element.65), channel_id=1, source_target_pairs={{0,2},{1,3},{2,0},{3,1},{4,6},{5,7},{6,4},{7,5},{8,10},{9,11},{10,... | collective-permute-start | bytes 786440 | tf_op jit(solution)/shard_map/ppermute | solution.py:525
  56.9 0.6 collective-permute-start.15
  57.5 5.8 %back_own.1 = (bf16[256,1024]{1,0:T(8,128)(2,1)}, f32[2,256,1024]{2,1,0:T(8,128)S(1)}) custom-call(s32[2]{0:T(128)S(1)} %copy-done.6, s32[8]{0:T(128)S(1)} %reshape_squeeze.3.lists, bf16[256,1024]{1,0:T(8,128)(2,1)S(1)} %bitcast.33, bf16[256,1024]{1,0:T(8,128)(2,1)S(1)} %bitcast.26, bf16[256,1024]{1,0:T(8,128)(2,1)S(1)} %bitcast.29, ...), custom_call_target="tpu_custom_call" | custom-call | flops 6000000000 | bytes 16777216 | tf_op jit(solution)/shard_map/back_own/pallas_call | solution.py:459
  63.3 0.5 collective-permute-done.13.t1
  63.7 1.5 %collective-permute-done.14.t2 = bf16[2,64,1024]{2,1,0:T(8,128)(2,1)S(1)} collective-permute-done((bf16[2,64,1024]{2,1,0:T(8,128)(2,1)S(1)}, bf16[2,64,1024]{2,1,0:T(8,128)(2,1)S(1)}, u32[]{:S(2)}, u32[]{:S(2)}) %collective-permute-start.14) | collective-permute-done | bytes 262176 | tf_op jit(solution)/shard_map/ppermute | solution.py:525
  65.2 4.6 %collective-permute-done.15.t3 = bf16[2,64,1024]{2,1,0:T(8,128)(2,1)S(1)} collective-permute-done((bf16[2,64,1024]{2,1,0:T(8,128)(2,1)S(1)}, bf16[2,64,1024]{2,1,0:T(8,128)(2,1)S(1)}, u32[]{:S(2)}, u32[]{:S(2)}) %collective-permute-start.15) | collective-permute-done | bytes 262176 | tf_op jit(solution)/shard_map/ppermute | solution.py:525
  69.8 1.6 %finish_time.1 = (bf16[256,1024]{1,0:T(8,128)(2,1)}, bf16[256,1024]{1,0:T(8,128)(2,1)}) custom-call(s32[2]{0:T(128)S(1)} %copy-done.6, bf16[2,64,1024]{2,1,0:T(8,128)(2,1)S(1)} %get-tuple-element.56.after.t0, bf16[2,64,1024]{2,1,0:T(8,128)(2,1)S(1)} %collective-permute-done.13.t1, bf16[2,64,1024]{2,1,0:T(8,128)(2,1)S(1)} %collective-permute-done.14.t2, ...), custom_call_target="tpu_custom_call" | custom-call | bytes 2097152 | tf_op jit(solution)/shard_map/finish_time/pallas_call | solution.py:482
  71.4 0.0 collective-permute-done.11.low
  71.4 0.0 collective-permute-done.12.high
  71.4 1.2 %finish.1 = (bf16[256,1024]{1,0:T(8,128)(2,1)}, bf16[256,1024]{1,0:T(8,128)(2,1)}) custom-call(f32[2,256,1024]{2,1,0:T(8,128)S(1)} %get-tuple-element.59.totals, bf16[2,256,1024]{2,1,0:T(8,128)(2,1)S(1)} %collective-permute-done.11.low, bf16[2,256,1024]{2,1,0:T(8,128)(2,1)S(1)} %collective-permute-done.12.high), custom_call_target="tpu_custom_call" | custom-call | bytes 5242880 | tf_op jit(solution)/shard_map/finish/pallas_call | solution.py:499
  (4 shorter events, 0.0 us)
Async XLA Ops:
  0.6 11.4 %copy-start = (s32[64,2,4,2]{0,3,2,1:T(2,128)S(1)}, s32[64,2,4,2]{0,3,2,1:T(2,128)}, u32[]{:S(2)}) copy-start(s32[64,2,4,2]{0,3,2,1:T(2,128)} %param.17) | copy-start | bytes 12292
  0.6 11.7 %copy-start.5 = (bf16[1,256,1024]{2,1,0:T(8,128)(2,1)S(1)}, bf16[1,256,1024]{2,1,0:T(8,128)(2,1)}, u32[]{:S(2)}) copy-start(bf16[1,256,1024]{2,1,0:T(8,128)(2,1)} %param.11) | copy-start | bytes 1572868
  0.7 11.7 %copy-start.4 = (bf16[1,256,1024]{2,1,0:T(8,128)(2,1)S(1)}, bf16[1,256,1024]{2,1,0:T(8,128)(2,1)}, u32[]{:S(2)}) copy-start(bf16[1,256,1024]{2,1,0:T(8,128)(2,1)} %param.10) | copy-start | bytes 1572868
  0.7 11.7 %copy-start.10 = (s32[128]{0:T(128)S(1)}, s32[128]{0:T(128)}, u32[]{:S(2)}) copy-start(s32[128]{0:T(128)} %fluid.3) | copy-start | bytes 1540
  0.7 11.7 %copy-start.9 = (s32[16384]{0:T(1024)S(1)}, s32[16384]{0:T(1024)}, u32[]{:S(2)}) copy-start(s32[16384]{0:T(1024)} %param.16) | copy-start | bytes 196612
  1.3 11.1 %copy-start.6 = (s32[2]{0:T(128)S(1)}, s32[2]{0:T(128)}, u32[]{:S(2)}) copy-start(s32[2]{0:T(128)} %pad_add_fusion.place) | copy-start | bytes 28
  4.8 15.5 %collective-permute-start.1 = (bf16[2,256,1024]{2,1,0:T(8,128)(2,1)}, bf16[2,256,1024]{2,1,0:T(8,128)(2,1)S(1)}, u32[]{:S(2)}, u32[]{:S(2)}) collective-permute-start(bf16[2,256,1024]{2,1,0:T(8,128)(2,1)} %get-tuple-element.37), channel_id=1, source_target_pairs={{0,4},{4,8},{8,12},{12,16},{16,20},{20,24},{24,28},{28,32},{32,36}... | collective-permute-start | bytes 3145736 | tf_op jit(solution)/shard_map/ppermute | solution.py:531
  8.3 15.9 %collective-permute-start = (bf16[2,256,1024]{2,1,0:T(8,128)(2,1)}, bf16[2,256,1024]{2,1,0:T(8,128)(2,1)}, u32[]{:S(2)}, u32[]{:S(2)}) collective-permute-start(bf16[2,256,1024]{2,1,0:T(8,128)(2,1)} %get-tuple-element.37), channel_id=1, source_target_pairs={{0,252},{4,0},{8,4},{12,8},{16,12},{20,16},{24,20},{28,24},{32,28}... | collective-permute-start | bytes 3145736 | tf_op jit(solution)/shard_map/ppermute | solution.py:531
  8.3 25.7 %collective-permute-start.2 = (bf16[3,64,1024]{2,1,0:T(8,128)(2,1)}, bf16[3,64,1024]{2,1,0:T(8,128)(2,1)S(1)}, u32[]{:S(2)}, u32[]{:S(2)}) collective-permute-start(bf16[3,64,1024]{2,1,0:T(8,128)(2,1)} %get-tuple-element.44), channel_id=1, source_target_pairs={{0,3},{1,0},{2,1},{3,2},{4,7},{5,4},{6,5},{7,6},{8,11},{9,8},{10,9... | collective-permute-start | bytes 1179656 | tf_op jit(solution)/shard_map/ppermute | solution.py:525
  11.0 23.5 %collective-permute-start.3 = (bf16[3,64,1024]{2,1,0:T(8,128)(2,1)}, bf16[3,64,1024]{2,1,0:T(8,128)(2,1)S(1)}, u32[]{:S(2)}, u32[]{:S(2)}) collective-permute-start(bf16[3,64,1024]{2,1,0:T(8,128)(2,1)} %get-tuple-element.45), channel_id=1, source_target_pairs={{0,2},{1,3},{2,0},{3,1},{4,6},{5,7},{6,4},{7,5},{8,10},{9,11},{10,... | collective-permute-start | bytes 1179656 | tf_op jit(solution)/shard_map/ppermute | solution.py:525
  11.3 23.2 %collective-permute-start.4 = (bf16[3,64,1024]{2,1,0:T(8,128)(2,1)}, bf16[3,64,1024]{2,1,0:T(8,128)(2,1)S(1)}, u32[]{:S(2)}, u32[]{:S(2)}) collective-permute-start(bf16[3,64,1024]{2,1,0:T(8,128)(2,1)} %get-tuple-element.46), channel_id=1, source_target_pairs={{0,1},{1,2},{2,3},{3,0},{4,5},{5,6},{6,7},{7,4},{8,9},{9,10},{10,1... | collective-permute-start | bytes 1179656 | tf_op jit(solution)/shard_map/ppermute | solution.py:525
  12.4 1.0 %copy-start.7 = (bf16[1,256,1024]{2,1,0:T(8,128)(2,1)S(1)}, bf16[1,256,1024]{2,1,0:T(8,128)(2,1)}, u32[]{:S(2)}) copy-start(bf16[1,256,1024]{2,1,0:T(8,128)(2,1)} %param.9) | copy-start | bytes 1572868
  13.4 10.8 %copy-start.8 = (bf16[1,256,1024]{2,1,0:T(8,128)(2,1)S(1)}, bf16[1,256,1024]{2,1,0:T(8,128)(2,1)}, u32[]{:S(2)}) copy-start(bf16[1,256,1024]{2,1,0:T(8,128)(2,1)} %param.9) | copy-start | bytes 1572868
  24.2 10.3 %copy-start.1 = (bf16[1,256,1024]{2,1,0:T(8,128)(2,1)S(1)}, bf16[1,256,1024]{2,1,0:T(8,128)(2,1)}, u32[]{:S(2)}) copy-start(bf16[1,256,1024]{2,1,0:T(8,128)(2,1)} %param.12) | copy-start | bytes 1572868
  24.2 10.3 %copy-start.2 = (bf16[1,256,1024]{2,1,0:T(8,128)(2,1)S(1)}, bf16[1,256,1024]{2,1,0:T(8,128)(2,1)}, u32[]{:S(2)}) copy-start(bf16[1,256,1024]{2,1,0:T(8,128)(2,1)} %param.13) | copy-start | bytes 1572868
  24.2 10.3 %copy-start.3 = (bf16[1,256,1024]{2,1,0:T(8,128)(2,1)S(1)}, bf16[1,256,1024]{2,1,0:T(8,128)(2,1)}, u32[]{:S(2)}) copy-start(bf16[1,256,1024]{2,1,0:T(8,128)(2,1)} %param.14) | copy-start | bytes 1572868
  30.8 10.8 %collective-permute-start.8 = (bf16[64,1024]{1,0:T(8,128)(2,1)S(1)}, bf16[64,1024]{1,0:T(8,128)(2,1)S(1)}, u32[]{:S(2)}, u32[]{:S(2)}) collective-permute-start(bf16[64,1024]{1,0:T(8,128)(2,1)S(1)} %get-tuple-element.53), channel_id=1, source_target_pairs={{0,3},{1,0},{2,1},{3,2},{4,7},{5,4},{6,5},{7,6},{8,11},{9,8},{10,9... | collective-permute-start | bytes 393224 | tf_op jit(solution)/shard_map/ppermute | solution.py:525
  33.6 8.0 %collective-permute-start.9 = (bf16[64,1024]{1,0:T(8,128)(2,1)S(1)}, bf16[64,1024]{1,0:T(8,128)(2,1)S(1)}, u32[]{:S(2)}, u32[]{:S(2)}) collective-permute-start(bf16[64,1024]{1,0:T(8,128)(2,1)S(1)} %get-tuple-element.54), channel_id=1, source_target_pairs={{0,2},{1,3},{2,0},{3,1},{4,6},{5,7},{6,4},{7,5},{8,10},{9,11},{10,... | collective-permute-start | bytes 393224 | tf_op jit(solution)/shard_map/ppermute | solution.py:525
  33.9 7.8 %collective-permute-start.10 = (bf16[64,1024]{1,0:T(8,128)(2,1)S(1)}, bf16[64,1024]{1,0:T(8,128)(2,1)S(1)}, u32[]{:S(2)}, u32[]{:S(2)}) collective-permute-start(bf16[64,1024]{1,0:T(8,128)(2,1)S(1)} %get-tuple-element.55), channel_id=1, source_target_pairs={{0,1},{1,2},{2,3},{3,0},{4,5},{5,6},{6,7},{7,4},{8,9},{9,10},{10,1... | collective-permute-start | bytes 393224 | tf_op jit(solution)/shard_map/ppermute | solution.py:525
  38.0 7.2 %collective-permute-start.5 = (bf16[64,1024]{1,0:T(8,128)(2,1)S(1)}, bf16[64,1024]{1,0:T(8,128)(2,1)S(1)}, u32[]{:S(2)}, u32[]{:S(2)}) collective-permute-start(bf16[64,1024]{1,0:T(8,128)(2,1)S(1)} %get-tuple-element.49), channel_id=1, source_target_pairs={{0,3},{1,0},{2,1},{3,2},{4,7},{5,4},{6,5},{7,6},{8,11},{9,8},{10,9... | collective-permute-start | bytes 393224 | tf_op jit(solution)/shard_map/ppermute | solution.py:525
  40.2 5.7 %collective-permute-start.6 = (bf16[64,1024]{1,0:T(8,128)(2,1)S(1)}, bf16[64,1024]{1,0:T(8,128)(2,1)S(1)}, u32[]{:S(2)}, u32[]{:S(2)}) collective-permute-start(bf16[64,1024]{1,0:T(8,128)(2,1)S(1)} %get-tuple-element.50), channel_id=1, source_target_pairs={{0,2},{1,3},{2,0},{3,1},{4,6},{5,7},{6,4},{7,5},{8,10},{9,11},{10,... | collective-permute-start | bytes 393224 | tf_op jit(solution)/shard_map/ppermute | solution.py:525
  41.7 5.5 %collective-permute-start.7 = (bf16[64,1024]{1,0:T(8,128)(2,1)S(1)}, bf16[64,1024]{1,0:T(8,128)(2,1)S(1)}, u32[]{:S(2)}, u32[]{:S(2)}) collective-permute-start(bf16[64,1024]{1,0:T(8,128)(2,1)S(1)} %get-tuple-element.51), channel_id=1, source_target_pairs={{0,1},{1,2},{2,3},{3,0},{4,5},{5,6},{6,7},{7,4},{8,9},{9,10},{10,1... | collective-permute-start | bytes 393224 | tf_op jit(solution)/shard_map/ppermute | solution.py:525
  52.4 18.9 %collective-permute-start.11 = (bf16[2,256,1024]{2,1,0:T(8,128)(2,1)S(1)}, bf16[2,256,1024]{2,1,0:T(8,128)(2,1)S(1)}, u32[]{:S(2)}, u32[]{:S(2)}) collective-permute-start(bf16[2,256,1024]{2,1,0:T(8,128)(2,1)S(1)} %get-tuple-element.60), channel_id=1, source_target_pairs={{0,4},{4,8},{8,12},{12,16},{16,20},{20,24},{24,28},{28,32},{32,36}... | collective-permute-start | bytes 3145736 | tf_op jit(solution)/shard_map/ppermute | solution.py:548
  55.3 16.0 %collective-permute-start.12 = (bf16[2,256,1024]{2,1,0:T(8,128)(2,1)S(1)}, bf16[2,256,1024]{2,1,0:T(8,128)(2,1)S(1)}, u32[]{:S(2)}, u32[]{:S(2)}) collective-permute-start(bf16[2,256,1024]{2,1,0:T(8,128)(2,1)S(1)} %get-tuple-element.61), channel_id=1, source_target_pairs={{0,252},{4,0},{8,4},{12,8},{16,12},{20,16},{24,20},{28,24},{32,28}... | collective-permute-start | bytes 3145736 | tf_op jit(solution)/shard_map/ppermute | solution.py:547
  55.3 8.4 %collective-permute-start.13 = (bf16[2,64,1024]{2,1,0:T(8,128)(2,1)S(1)}, bf16[2,64,1024]{2,1,0:T(8,128)(2,1)S(1)}, u32[]{:S(2)}, u32[]{:S(2)}) collective-permute-start(bf16[2,64,1024]{2,1,0:T(8,128)(2,1)S(1)} %get-tuple-element.64), channel_id=1, source_target_pairs={{0,3},{1,0},{2,1},{3,2},{4,7},{5,4},{6,5},{7,6},{8,11},{9,8},{10,9... | collective-permute-start | bytes 786440 | tf_op jit(solution)/shard_map/ppermute | solution.py:525
  55.6 9.6 %collective-permute-start.14 = (bf16[2,64,1024]{2,1,0:T(8,128)(2,1)S(1)}, bf16[2,64,1024]{2,1,0:T(8,128)(2,1)S(1)}, u32[]{:S(2)}, u32[]{:S(2)}) collective-permute-start(bf16[2,64,1024]{2,1,0:T(8,128)(2,1)S(1)} %get-tuple-element.65), channel_id=1, source_target_pairs={{0,2},{1,3},{2,0},{3,1},{4,6},{5,7},{6,4},{7,5},{8,10},{9,11},{10,... | collective-permute-start | bytes 786440 | tf_op jit(solution)/shard_map/ppermute | solution.py:525
  56.9 12.9 %collective-permute-start.15 = (bf16[2,64,1024]{2,1,0:T(8,128)(2,1)S(1)}, bf16[2,64,1024]{2,1,0:T(8,128)(2,1)S(1)}, u32[]{:S(2)}, u32[]{:S(2)}) collective-permute-start(bf16[2,64,1024]{2,1,0:T(8,128)(2,1)S(1)} %get-tuple-element.66), channel_id=1, source_target_pairs={{0,1},{1,2},{2,3},{3,0},{4,5},{5,6},{6,7},{7,4},{8,9},{9,10},{10,1... | collective-permute-start | bytes 786440 | tf_op jit(solution)/shard_map/ppermute | solution.py:525

commit v3 on v2

--- a/solution.py
+++ b/solution.py
@@ -287,7 +287,7 @@
         for u in range(4):
             outs[u][rows, lanes] = sums[u].astype(BF16)
 
-    pl.loop(0, 16, unroll=4)(tile)
+    pl.loop(0, 16, unroll=8)(tile)
 
 
 def time_first(place, q, k, g, m1, m2, m3, after):
@@ -333,7 +333,7 @@
         for u in range(4):
             outs[u][1, rows, lanes] = (key_sums[u] * SCALE).astype(BF16)
 
-    pl.loop(0, 16, unroll=4)(tile)
+    pl.loop(0, 16, unroll=8)(tile)
 
 
 def time_second(place, q, k, g, m1, m2, m3, attn, x0, x1, x2, x3):
@@ -471,19 +471,25 @@
     )(place, lists, q, k, v, high, low, weights, factors, states_t, slopes, *pieces)
 
 
-def finish_time_kernel(place, t0, t1, t2, t3, query_t, key_t):
+def finish_time_kernel(place, t0, t1, t2, t3, query_t, key_t, sems):
+    copies = []
     for d, piece in enumerate((t0, t1, t2, t3)):
-        start = pl.multiple_of(lax.rem(place[0] + d, 4) * QUARTER, QUARTER)
-        query_t[pl.ds(start, QUARTER), :] = piece[0]
-        key_t[pl.ds(start, QUARTER), :] = piece[1]
+        rows = pl.ds(pl.multiple_of(lax.rem(place[0] + d, 4) * QUARTER, QUARTER), QUARTER)
+        for n, out in enumerate((query_t, key_t)):
+            copies.append(pltpu.make_async_copy(piece.at[n], out.at[rows, :], sems.at[2 * d + n]))
+    for copy in copies:
+        copy.start()
+    for copy in copies:
+        copy.wait()
 
 
 def finish_time(place, pieces):
     return pl.pallas_call(
         finish_time_kernel,
         in_specs=[SMEM_SPEC] + [VMEM_SPEC] * 4,
-        out_specs=[VMEM_SPEC] * 2,
+        out_specs=[HBM_SPEC] * 2,
         out_shape=[jax.ShapeDtypeStruct((TOK, D), BF16)] * 2,
+        scratch_shapes=[pltpu.SemaphoreType.DMA((8,))],
         compiler_params=kernel_params(24),
         cost_estimate=cost(0, 2 << 20),
         name="finish_time",

time: 73.5 us -> 73.3 us (level)
  no operation moved by 1% of the time
where the time goes in v3:
time: 73.3 us; the launch traced here: 72.4 us
  Pallas kernels  34.2 us (47%)
  starting transfers between devices  19.7 us (27%)
  waiting for transfers between devices  15.7 us (21%)
  local copies, waits for them, and re-layouts  1.38 us (2%)
  between operations  0.84 us (1%)
    ppermute x12, starting transfers between devices, shift(): return lax.ppermute(x, 'tm', [(i, (i + d) % steps) for i in range(steps)])  13.3 us
    ppermute x12, waiting for transfers between devices, shift(): return lax.ppermute(x, 'tm', [(i, (i + d) % steps) for i in range(steps)])  8.57 us
    ppermute x2, waiting for transfers between devices, body(): low, high = (lax.ppermute(kv, 'space', up), lax.ppermute(kv, 'space', down))  7.13 us
    pallas_call x1, Pallas kernels, forward_sides(): pl.pallas_call(forward_sides_kernel, in_specs=[SMEM_SPEC] * 3 + [VMEM_SPE...  6.62 us
    pallas_call x1, Pallas kernels, back_own(): pl.pallas_call(back_own_kernel, in_specs=[SMEM_SPEC] * 2 + [VMEM_SPEC] *...  5.75 us
    pallas_call x1, Pallas kernels, back_sides(): pl.pallas_call(back_sides_kernel, in_specs=[SMEM_SPEC] * 2 + [VMEM_SPEC]...  5.25 us
    pallas_call x1, Pallas kernels, forward_own(): pl.pallas_call(forward_own_kernel, in_specs=[SMEM_SPEC] * 2 + [VMEM_SPEC]...  3.64 us
    pallas_call x1, Pallas kernels, time_second(): pl.pallas_call(time_second_kernel, in_specs=[SMEM_SPEC] + [VMEM_SPEC] * 1...  3.49 us
  transfers between devices with their start and end apart: 16, of which 7 were waited for; matrix products, arithmetic and copies ran while one was open for 0% of the time, Pallas kernels for 34%

profile of v3, /device:TPU:103, one launch (start us, length us, event | category | flops | bytes accessed | tf_op | source)
XLA Modules:
  0.0 72.4 jit_solution(3350399490880530278)
XLA Ops:
  0.6 0.0 copy-start
  0.6 0.0 copy-start.5
  0.7 0.0 copy-start.4
  0.7 0.0 copy-start.10
  0.7 0.0 copy-start.9
  0.7 0.6 pad_add_fusion.place
  1.3 0.0 copy-start.6
  1.3 3.5 %stage.1 = (bf16[3,64,1024]{2,1,0:T(8,128)(2,1)}, bf16[3,64,1024]{2,1,0:T(8,128)(2,1)}, bf16[3,64,1024]{2,1,0:T(8,128)(2,1)}, bf16[2,256,1024]{2,1,0:T(8,128)(2,1)}) custom-call(s32[2]{0:T(128)} %pad_add_fusion.place, bf16[256,1024]{1,0:T(8,128)(2,1)} %bitcast.15, bf16[256,1024]{1,0:T(8,128)(2,1)} %bitcast.18, bf16[256,1024]{1,0:T(8,128)(2,1)} %bitcast.21, ...), custom_call_target="tpu_custom_call" | custom-call | bytes 4194304 | tf_op jit(solution)/shard_map/stage/pallas_call | solution.py:92
  4.8 3.5 %collective-permute-start.1 = (bf16[2,256,1024]{2,1,0:T(8,128)(2,1)}, bf16[2,256,1024]{2,1,0:T(8,128)(2,1)S(1)}, u32[]{:S(2)}, u32[]{:S(2)}) collective-permute-start(bf16[2,256,1024]{2,1,0:T(8,128)(2,1)} %get-tuple-element.37), channel_id=1, source_target_pairs={{0,4},{4,8},{8,12},{12,16},{16,20},{20,24},{24,28},{28,32},{32,36}... | collective-permute-start | bytes 3145736 | tf_op jit(solution)/shard_map/ppermute | solution.py:537
  8.3 0.0 collective-permute-start
  8.3 2.7 %collective-permute-start.2 = (bf16[3,64,1024]{2,1,0:T(8,128)(2,1)}, bf16[3,64,1024]{2,1,0:T(8,128)(2,1)S(1)}, u32[]{:S(2)}, u32[]{:S(2)}) collective-permute-start(bf16[3,64,1024]{2,1,0:T(8,128)(2,1)} %get-tuple-element.44), channel_id=1, source_target_pairs={{0,3},{1,0},{2,1},{3,2},{4,7},{5,4},{6,5},{7,6},{8,11},{9,8},{10,9... | collective-permute-start | bytes 1179656 | tf_op jit(solution)/shard_map/ppermute | solution.py:531
  11.0 0.3 collective-permute-start.3
  11.3 0.7 collective-permute-start.4
  12.0 0.0 copy-done
  12.0 0.1 constant_dynamic-slice_fusion
  12.1 0.1 copy.14
  12.2 0.1 reshape_squeeze.3.lists
  12.3 0.0 copy-done.5
  12.3 0.0 copy-done.4
  12.3 0.0 copy-done.10
  12.3 0.0 copy-done.9
  12.4 0.0 copy-done.6
  12.4 0.0 copy-start.7
  12.4 1.0 %copy-done.7 = bf16[1,256,1024]{2,1,0:T(8,128)(2,1)S(1)} copy-done((bf16[1,256,1024]{2,1,0:T(8,128)(2,1)S(1)}, bf16[1,256,1024]{2,1,0:T(8,128)(2,1)}, u32[]{:S(2)}) %copy-start.7) | copy-done | bytes 524312
  13.4 0.0 copy-start.8
  13.4 3.6 %forward_own.1 = (bf16[8,256,512]{2,1,0:T(8,128)(2,1)S(1)}, f32[8,8,512]{2,1,0:T(8,128)S(1)}, f32[1024,256]{1,0:T(8,128)S(1)}) custom-call(s32[2]{0:T(128)S(1)} %copy-done.6, s32[128]{0:T(128)S(1)} %copy-done.10, s32[128,128]{1,0:T(8,128)S(1)} %bitcast.34, bf16[256,1024]{1,0:T(8,128)(2,1)S(1)} %bitcast.30, bf16[256,1024]{1,0:T(8,128)(2,1)S(1)} %bitcast.25, ...), custom_call_target="tpu_custom_call" | custom-call | flops 2000000000 | bytes 8388608 | tf_op jit(solution)/shard_map/forward_own/pallas_call | solution.py:160
  17.1 3.3 %collective-permute-done.1.low.from_low = bf16[2,256,1024]{2,1,0:T(8,128)(2,1)S(1)} collective-permute-done((bf16[2,256,1024]{2,1,0:T(8,128)(2,1)}, bf16[2,256,1024]{2,1,0:T(8,128)(2,1)S(1)}, u32[]{:S(2)}, u32[]{:S(2)}) %collective-permute-start.1) | collective-permute-done | bytes 1048608 | tf_op jit(solution)/shard_map/ppermute | solution.py:537
  20.3 3.9 %collective-permute-done.high.from_high = bf16[2,256,1024]{2,1,0:T(8,128)(2,1)} collective-permute-done((bf16[2,256,1024]{2,1,0:T(8,128)(2,1)}, bf16[2,256,1024]{2,1,0:T(8,128)(2,1)}, u32[]{:S(2)}, u32[]{:S(2)}) %collective-permute-start) | collective-permute-done | bytes 1048608 | tf_op jit(solution)/shard_map/ppermute | solution.py:537
  24.2 0.0 copy-done.8
  24.2 6.6 %forward_sides.1 = (bf16[64,1024]{1,0:T(8,128)(2,1)S(1)}, bf16[64,1024]{1,0:T(8,128)(2,1)S(1)}, bf16[64,1024]{1,0:T(8,128)(2,1)S(1)}, bf16[64,1024]{1,0:T(8,128)...) custom-call(s32[2]{0:T(128)S(1)} %copy-done.6, ...), custom_call_target="tpu_custom_call" | custom-call | flops 2000000000 | bytes 8388608 | tf_op jit(solution)/shard_map/forward_sides/pallas_call | solution.py:230
  30.8 2.8 %collective-permute-start.8 = (bf16[64,1024]{1,0:T(8,128)(2,1)S(1)}, bf16[64,1024]{1,0:T(8,128)(2,1)S(1)}, u32[]{:S(2)}, u32[]{:S(2)}) collective-permute-start(bf16[64,1024]{1,0:T(8,128)(2,1)S(1)} %get-tuple-element.53), channel_id=1, source_target_pairs={{0,3},{1,0},{2,1},{3,2},{4,7},{5,4},{6,5},{7,6},{8,11},{9,8},{10,9... | collective-permute-start | bytes 393224 | tf_op jit(solution)/shard_map/ppermute | solution.py:531
  33.6 0.3 collective-permute-start.9
  33.9 0.0 collective-permute-done.2.m1
  33.9 0.6 collective-permute-start.10
  34.5 0.0 collective-permute-done.3.m2
  34.5 0.0 collective-permute-done.4.m3
  34.5 0.0 copy-done.1
  34.5 0.0 copy-done.2
  34.5 0.0 copy-done.3
  34.5 3.2 %time_first.1 = (bf16[64,1024]{1,0:T(8,128)(2,1)S(1)}, bf16[64,1024]{1,0:T(8,128)(2,1)S(1)}, bf16[64,1024]{1,0:T(8,128)(2,1)S(1)}, bf16[64,1024]{1,0:T(8,128)(2,1)S(1)}, bf16[16,64,1024]{2,1,0:T(8,128)(2,1)S(1)}) custom-call(s32[2]{0:T(128)S(1)} %copy-done.6, bf16[256,1024]{1,0:T(8,128)(2,1)S(1)} %bitcast.16, bf16[256,1024]{1,0:T(8,128)(2,1)S(1)} %bitcast.19, ...), custom_call_target="tpu_custom_call" | custom-call | flops 1000000000 | bytes 8388608 | tf_op jit(solution)/shard_map/time_first/pallas_call | solution.py:295
  37.8 2.2 %collective-permute-start.5 = (bf16[64,1024]{1,0:T(8,128)(2,1)S(1)}, bf16[64,1024]{1,0:T(8,128)(2,1)S(1)}, u32[]{:S(2)}, u32[]{:S(2)}) collective-permute-start(bf16[64,1024]{1,0:T(8,128)(2,1)S(1)} %get-tuple-element.49), channel_id=1, source_target_pairs={{0,3},{1,0},{2,1},{3,2},{4,7},{5,4},{6,5},{7,6},{8,11},{9,8},{10,9... | collective-permute-start | bytes 393224 | tf_op jit(solution)/shard_map/ppermute | solution.py:531
  40.0 1.5 %collective-permute-start.6 = (bf16[64,1024]{1,0:T(8,128)(2,1)S(1)}, bf16[64,1024]{1,0:T(8,128)(2,1)S(1)}, u32[]{:S(2)}, u32[]{:S(2)}) collective-permute-start(bf16[64,1024]{1,0:T(8,128)(2,1)S(1)} %get-tuple-element.50), channel_id=1, source_target_pairs={{0,2},{1,3},{2,0},{3,1},{4,6},{5,7},{6,4},{7,5},{8,10},{9,11},{10,... | collective-permute-start | bytes 393224 | tf_op jit(solution)/shard_map/ppermute | solution.py:531
  41.4 0.0 collective-permute-done.8.x1
  41.4 0.0 collective-permute-start.7
  41.5 0.0 collective-permute-done.9.x2
  41.5 0.0 collective-permute-done.10.x3
  41.5 3.5 %time_second.1 = (bf16[2,64,1024]{2,1,0:T(8,128)(2,1)S(1)}, bf16[2,64,1024]{2,1,0:T(8,128)(2,1)S(1)}, bf16[2,64,1024]{2,1,0:T(8,128)(2,1)S(1)}, bf16[2,64,1024]{2,1,0:T(8,128)(2,1)S(1)}) custom-call(s32[2]{0:T(128)S(1)} %copy-done.6, bf16[256,1024]{1,0:T(8,128)(2,1)S(1)} %bitcast.17, bf16[256,1024]{1,0:T(8,128)(2,1)S(1)} %bitcast.20, ...), custom_call_target="tpu_custom_call" | custom-call | flops 1000000000 | bytes 8388608 | tf_op jit(solution)/shard_map/time_second/pallas_call | solution.py:341
  45.0 0.0 collective-permute-done.5.g1
  45.0 0.6 collective-permute-done.6.g2
  45.6 1.4 %collective-permute-done.7.g3 = bf16[64,1024]{1,0:T(8,128)(2,1)S(1)} collective-permute-done((bf16[64,1024]{1,0:T(8,128)(2,1)S(1)}, bf16[64,1024]{1,0:T(8,128)(2,1)S(1)}, u32[]{:S(2)}, u32[]{:S(2)}) %collective-permute-start.7) | collective-permute-done | bytes 131104 | tf_op jit(solution)/shard_map/ppermute | solution.py:531
  47.0 5.2 %back_sides.1 = (bf16[2,256,1024]{2,1,0:T(8,128)(2,1)S(1)}, bf16[2,256,1024]{2,1,0:T(8,128)(2,1)S(1)}, bf16[8,256,512]{2,1,0:T(8,128)(2,1)S(1)}) custom-call(s32[2]{0:T(128)S(1)} %copy-done.6, s32[8]{0:T(128)S(1)} %reshape_squeeze.3.lists, bf16[256,1024]{1,0:T(8,128)(2,1)S(1)} %bitcast.32, bf16[2,256,1024]{2,1,0:T(8,128)(2,1)S(1)} %collective-permute-done.1.low.from_low, ...), custom_call_target="tpu_custom_call" | custom-call | flops 6000000000 | bytes 16777216 | tf_op jit(solution)/shard_map/back_sides/pallas_call | solution.py:407
  52.2 2.9 %collective-permute-start.11 = (bf16[2,256,1024]{2,1,0:T(8,128)(2,1)S(1)}, bf16[2,256,1024]{2,1,0:T(8,128)(2,1)S(1)}, u32[]{:S(2)}, u32[]{:S(2)}) collective-permute-start(bf16[2,256,1024]{2,1,0:T(8,128)(2,1)S(1)} %get-tuple-element.60), channel_id=1, source_target_pairs={{0,4},{4,8},{8,12},{12,16},{16,20},{20,24},{24,28},{28,32},{32,36}... | collective-permute-start | bytes 3145736 | tf_op jit(solution)/shard_map/ppermute | solution.py:554
  55.1 0.0 collective-permute-start.12
  55.1 0.3 collective-permute-start.13
  55.4 1.3 %collective-permute-start.14 = (bf16[2,64,1024]{2,1,0:T(8,128)(2,1)S(1)}, bf16[2,64,1024]{2,1,0:T(8,128)(2,1)S(1)}, u32[]{:S(2)}, u32[]{:S(2)}) collective-permute-start(bf16[2,64,1024]{2,1,0:T(8,128)(2,1)S(1)} %get-tuple-element.65), channel_id=1, source_target_pairs={{0,2},{1,3},{2,0},{3,1},{4,6},{5,7},{6,4},{7,5},{8,10},{9,11},{10,... | collective-permute-start | bytes 786440 | tf_op jit(solution)/shard_map/ppermute | solution.py:531
  56.7 0.6 collective-permute-start.15
  57.3 5.8 %back_own.1 = (bf16[256,1024]{1,0:T(8,128)(2,1)}, f32[2,256,1024]{2,1,0:T(8,128)S(1)}) custom-call(s32[2]{0:T(128)S(1)} %copy-done.6, s32[8]{0:T(128)S(1)} %reshape_squeeze.3.lists, bf16[256,1024]{1,0:T(8,128)(2,1)S(1)} %bitcast.33, bf16[256,1024]{1,0:T(8,128)(2,1)S(1)} %bitcast.26, bf16[256,1024]{1,0:T(8,128)(2,1)S(1)} %bitcast.29, ...), custom_call_target="tpu_custom_call" | custom-call | flops 6000000000 | bytes 16777216 | tf_op jit(solution)/shard_map/back_own/pallas_call | solution.py:459
  63.0 0.5 collective-permute-done.13.t1
  63.5 1.5 %collective-permute-done.14.t2 = bf16[2,64,1024]{2,1,0:T(8,128)(2,1)S(1)} collective-permute-done((bf16[2,64,1024]{2,1,0:T(8,128)(2,1)S(1)}, bf16[2,64,1024]{2,1,0:T(8,128)(2,1)S(1)}, u32[]{:S(2)}, u32[]{:S(2)}) %collective-permute-start.14) | collective-permute-done | bytes 262176 | tf_op jit(solution)/shard_map/ppermute | solution.py:531
  65.0 4.6 %collective-permute-done.15.t3 = bf16[2,64,1024]{2,1,0:T(8,128)(2,1)S(1)} collective-permute-done((bf16[2,64,1024]{2,1,0:T(8,128)(2,1)S(1)}, bf16[2,64,1024]{2,1,0:T(8,128)(2,1)S(1)}, u32[]{:S(2)}, u32[]{:S(2)}) %collective-permute-start.15) | collective-permute-done | bytes 262176 | tf_op jit(solution)/shard_map/ppermute | solution.py:531
  69.6 1.6 %finish_time.1 = (bf16[256,1024]{1,0:T(8,128)(2,1)}, bf16[256,1024]{1,0:T(8,128)(2,1)}) custom-call(s32[2]{0:T(128)S(1)} %copy-done.6, bf16[2,64,1024]{2,1,0:T(8,128)(2,1)S(1)} %get-tuple-element.56.after.t0, bf16[2,64,1024]{2,1,0:T(8,128)(2,1)S(1)} %collective-permute-done.13.t1, bf16[2,64,1024]{2,1,0:T(8,128)(2,1)S(1)} %collective-permute-done.14.t2, ...), custom_call_target="tpu_custom_call" | custom-call | bytes 2097152 | tf_op jit(solution)/shard_map/finish_time/pallas_call | solution.py:487
  71.2 0.0 collective-permute-done.11.low
  71.2 0.0 collective-permute-done.12.high
  71.2 1.2 %finish.1 = (bf16[256,1024]{1,0:T(8,128)(2,1)}, bf16[256,1024]{1,0:T(8,128)(2,1)}) custom-call(f32[2,256,1024]{2,1,0:T(8,128)S(1)} %get-tuple-element.59.totals, bf16[2,256,1024]{2,1,0:T(8,128)(2,1)S(1)} %collective-permute-done.11.low, bf16[2,256,1024]{2,1,0:T(8,128)(2,1)S(1)} %collective-permute-done.12.high), custom_call_target="tpu_custom_call" | custom-call | bytes 5242880 | tf_op jit(solution)/shard_map/finish/pallas_call | solution.py:505
  (4 shorter events, 0.0 us)
Async XLA Ops:
  0.6 11.4 %copy-start = (s32[64,2,4,2]{0,3,2,1:T(2,128)S(1)}, s32[64,2,4,2]{0,3,2,1:T(2,128)}, u32[]{:S(2)}) copy-start(s32[64,2,4,2]{0,3,2,1:T(2,128)} %param.17) | copy-start | bytes 12292
  0.6 11.7 %copy-start.5 = (bf16[1,256,1024]{2,1,0:T(8,128)(2,1)S(1)}, bf16[1,256,1024]{2,1,0:T(8,128)(2,1)}, u32[]{:S(2)}) copy-start(bf16[1,256,1024]{2,1,0:T(8,128)(2,1)} %param.11) | copy-start | bytes 1572868
  0.7 11.7 %copy-start.4 = (bf16[1,256,1024]{2,1,0:T(8,128)(2,1)S(1)}, bf16[1,256,1024]{2,1,0:T(8,128)(2,1)}, u32[]{:S(2)}) copy-start(bf16[1,256,1024]{2,1,0:T(8,128)(2,1)} %param.10) | copy-start | bytes 1572868
  0.7 11.7 %copy-start.10 = (s32[128]{0:T(128)S(1)}, s32[128]{0:T(128)}, u32[]{:S(2)}) copy-start(s32[128]{0:T(128)} %fluid.3) | copy-start | bytes 1540
  0.7 11.7 %copy-start.9 = (s32[16384]{0:T(1024)S(1)}, s32[16384]{0:T(1024)}, u32[]{:S(2)}) copy-start(s32[16384]{0:T(1024)} %param.16) | copy-start | bytes 196612
  1.3 11.1 %copy-start.6 = (s32[2]{0:T(128)S(1)}, s32[2]{0:T(128)}, u32[]{:S(2)}) copy-start(s32[2]{0:T(128)} %pad_add_fusion.place) | copy-start | bytes 28
  4.8 15.5 %collective-permute-start.1 = (bf16[2,256,1024]{2,1,0:T(8,128)(2,1)}, bf16[2,256,1024]{2,1,0:T(8,128)(2,1)S(1)}, u32[]{:S(2)}, u32[]{:S(2)}) collective-permute-start(bf16[2,256,1024]{2,1,0:T(8,128)(2,1)} %get-tuple-element.37), channel_id=1, source_target_pairs={{0,4},{4,8},{8,12},{12,16},{16,20},{20,24},{24,28},{28,32},{32,36}... | collective-permute-start | bytes 3145736 | tf_op jit(solution)/shard_map/ppermute | solution.py:537
  8.3 15.9 %collective-permute-start = (bf16[2,256,1024]{2,1,0:T(8,128)(2,1)}, bf16[2,256,1024]{2,1,0:T(8,128)(2,1)}, u32[]{:S(2)}, u32[]{:S(2)}) collective-permute-start(bf16[2,256,1024]{2,1,0:T(8,128)(2,1)} %get-tuple-element.37), channel_id=1, source_target_pairs={{0,252},{4,0},{8,4},{12,8},{16,12},{20,16},{24,20},{28,24},{32,28}... | collective-permute-start | bytes 3145736 | tf_op jit(solution)/shard_map/ppermute | solution.py:537
  8.3 25.7 %collective-permute-start.2 = (bf16[3,64,1024]{2,1,0:T(8,128)(2,1)}, bf16[3,64,1024]{2,1,0:T(8,128)(2,1)S(1)}, u32[]{:S(2)}, u32[]{:S(2)}) collective-permute-start(bf16[3,64,1024]{2,1,0:T(8,128)(2,1)} %get-tuple-element.44), channel_id=1, source_target_pairs={{0,3},{1,0},{2,1},{3,2},{4,7},{5,4},{6,5},{7,6},{8,11},{9,8},{10,9... | collective-permute-start | bytes 1179656 | tf_op jit(solution)/shard_map/ppermute | solution.py:531
  11.0 23.5 %collective-permute-start.3 = (bf16[3,64,1024]{2,1,0:T(8,128)(2,1)}, bf16[3,64,1024]{2,1,0:T(8,128)(2,1)S(1)}, u32[]{:S(2)}, u32[]{:S(2)}) collective-permute-start(bf16[3,64,1024]{2,1,0:T(8,128)(2,1)} %get-tuple-element.45), channel_id=1, source_target_pairs={{0,2},{1,3},{2,0},{3,1},{4,6},{5,7},{6,4},{7,5},{8,10},{9,11},{10,... | collective-permute-start | bytes 1179656 | tf_op jit(solution)/shard_map/ppermute | solution.py:531
  11.3 23.2 %collective-permute-start.4 = (bf16[3,64,1024]{2,1,0:T(8,128)(2,1)}, bf16[3,64,1024]{2,1,0:T(8,128)(2,1)S(1)}, u32[]{:S(2)}, u32[]{:S(2)}) collective-permute-start(bf16[3,64,1024]{2,1,0:T(8,128)(2,1)} %get-tuple-element.46), channel_id=1, source_target_pairs={{0,1},{1,2},{2,3},{3,0},{4,5},{5,6},{6,7},{7,4},{8,9},{9,10},{10,1... | collective-permute-start | bytes 1179656 | tf_op jit(solution)/shard_map/ppermute | solution.py:531
  12.4 1.0 %copy-start.7 = (bf16[1,256,1024]{2,1,0:T(8,128)(2,1)S(1)}, bf16[1,256,1024]{2,1,0:T(8,128)(2,1)}, u32[]{:S(2)}) copy-start(bf16[1,256,1024]{2,1,0:T(8,128)(2,1)} %param.9) | copy-start | bytes 1572868
  13.4 10.8 %copy-start.8 = (bf16[1,256,1024]{2,1,0:T(8,128)(2,1)S(1)}, bf16[1,256,1024]{2,1,0:T(8,128)(2,1)}, u32[]{:S(2)}) copy-start(bf16[1,256,1024]{2,1,0:T(8,128)(2,1)} %param.9) | copy-start | bytes 1572868
  24.2 10.3 %copy-start.1 = (bf16[1,256,1024]{2,1,0:T(8,128)(2,1)S(1)}, bf16[1,256,1024]{2,1,0:T(8,128)(2,1)}, u32[]{:S(2)}) copy-start(bf16[1,256,1024]{2,1,0:T(8,128)(2,1)} %param.12) | copy-start | bytes 1572868
  24.2 10.3 %copy-start.2 = (bf16[1,256,1024]{2,1,0:T(8,128)(2,1)S(1)}, bf16[1,256,1024]{2,1,0:T(8,128)(2,1)}, u32[]{:S(2)}) copy-start(bf16[1,256,1024]{2,1,0:T(8,128)(2,1)} %param.13) | copy-start | bytes 1572868
  24.2 10.3 %copy-start.3 = (bf16[1,256,1024]{2,1,0:T(8,128)(2,1)S(1)}, bf16[1,256,1024]{2,1,0:T(8,128)(2,1)}, u32[]{:S(2)}) copy-start(bf16[1,256,1024]{2,1,0:T(8,128)(2,1)} %param.14) | copy-start | bytes 1572868
  30.8 10.6 %collective-permute-start.8 = (bf16[64,1024]{1,0:T(8,128)(2,1)S(1)}, bf16[64,1024]{1,0:T(8,128)(2,1)S(1)}, u32[]{:S(2)}, u32[]{:S(2)}) collective-permute-start(bf16[64,1024]{1,0:T(8,128)(2,1)S(1)} %get-tuple-element.53), channel_id=1, source_target_pairs={{0,3},{1,0},{2,1},{3,2},{4,7},{5,4},{6,5},{7,6},{8,11},{9,8},{10,9... | collective-permute-start | bytes 393224 | tf_op jit(solution)/shard_map/ppermute | solution.py:531
  33.6 7.8 %collective-permute-start.9 = (bf16[64,1024]{1,0:T(8,128)(2,1)S(1)}, bf16[64,1024]{1,0:T(8,128)(2,1)S(1)}, u32[]{:S(2)}, u32[]{:S(2)}) collective-permute-start(bf16[64,1024]{1,0:T(8,128)(2,1)S(1)} %get-tuple-element.54), channel_id=1, source_target_pairs={{0,2},{1,3},{2,0},{3,1},{4,6},{5,7},{6,4},{7,5},{8,10},{9,11},{10,... | collective-permute-start | bytes 393224 | tf_op jit(solution)/shard_map/ppermute | solution.py:531
  33.9 7.5 %collective-permute-start.10 = (bf16[64,1024]{1,0:T(8,128)(2,1)S(1)}, bf16[64,1024]{1,0:T(8,128)(2,1)S(1)}, u32[]{:S(2)}, u32[]{:S(2)}) collective-permute-start(bf16[64,1024]{1,0:T(8,128)(2,1)S(1)} %get-tuple-element.55), channel_id=1, source_target_pairs={{0,1},{1,2},{2,3},{3,0},{4,5},{5,6},{6,7},{7,4},{8,9},{9,10},{10,1... | collective-permute-start | bytes 393224 | tf_op jit(solution)/shard_map/ppermute | solution.py:531
  37.8 7.2 %collective-permute-start.5 = (bf16[64,1024]{1,0:T(8,128)(2,1)S(1)}, bf16[64,1024]{1,0:T(8,128)(2,1)S(1)}, u32[]{:S(2)}, u32[]{:S(2)}) collective-permute-start(bf16[64,1024]{1,0:T(8,128)(2,1)S(1)} %get-tuple-element.49), channel_id=1, source_target_pairs={{0,3},{1,0},{2,1},{3,2},{4,7},{5,4},{6,5},{7,6},{8,11},{9,8},{10,9... | collective-permute-start | bytes 393224 | tf_op jit(solution)/shard_map/ppermute | solution.py:531
  40.0 5.7 %collective-permute-start.6 = (bf16[64,1024]{1,0:T(8,128)(2,1)S(1)}, bf16[64,1024]{1,0:T(8,128)(2,1)S(1)}, u32[]{:S(2)}, u32[]{:S(2)}) collective-permute-start(bf16[64,1024]{1,0:T(8,128)(2,1)S(1)} %get-tuple-element.50), channel_id=1, source_target_pairs={{0,2},{1,3},{2,0},{3,1},{4,6},{5,7},{6,4},{7,5},{8,10},{9,11},{10,... | collective-permute-start | bytes 393224 | tf_op jit(solution)/shard_map/ppermute | solution.py:531
  41.4 5.5 %collective-permute-start.7 = (bf16[64,1024]{1,0:T(8,128)(2,1)S(1)}, bf16[64,1024]{1,0:T(8,128)(2,1)S(1)}, u32[]{:S(2)}, u32[]{:S(2)}) collective-permute-start(bf16[64,1024]{1,0:T(8,128)(2,1)S(1)} %get-tuple-element.51), channel_id=1, source_target_pairs={{0,1},{1,2},{2,3},{3,0},{4,5},{5,6},{6,7},{7,4},{8,9},{9,10},{10,1... | collective-permute-start | bytes 393224 | tf_op jit(solution)/shard_map/ppermute | solution.py:531
  52.2 19.0 %collective-permute-start.11 = (bf16[2,256,1024]{2,1,0:T(8,128)(2,1)S(1)}, bf16[2,256,1024]{2,1,0:T(8,128)(2,1)S(1)}, u32[]{:S(2)}, u32[]{:S(2)}) collective-permute-start(bf16[2,256,1024]{2,1,0:T(8,128)(2,1)S(1)} %get-tuple-element.60), channel_id=1, source_target_pairs={{0,4},{4,8},{8,12},{12,16},{16,20},{20,24},{24,28},{28,32},{32,36}... | collective-permute-start | bytes 3145736 | tf_op jit(solution)/shard_map/ppermute | solution.py:554
  55.1 16.1 %collective-permute-start.12 = (bf16[2,256,1024]{2,1,0:T(8,128)(2,1)S(1)}, bf16[2,256,1024]{2,1,0:T(8,128)(2,1)S(1)}, u32[]{:S(2)}, u32[]{:S(2)}) collective-permute-start(bf16[2,256,1024]{2,1,0:T(8,128)(2,1)S(1)} %get-tuple-element.61), channel_id=1, source_target_pairs={{0,252},{4,0},{8,4},{12,8},{16,12},{20,16},{24,20},{28,24},{32,28}... | collective-permute-start | bytes 3145736 | tf_op jit(solution)/shard_map/ppermute | solution.py:553
  55.1 8.4 %collective-permute-start.13 = (bf16[2,64,1024]{2,1,0:T(8,128)(2,1)S(1)}, bf16[2,64,1024]{2,1,0:T(8,128)(2,1)S(1)}, u32[]{:S(2)}, u32[]{:S(2)}) collective-permute-start(bf16[2,64,1024]{2,1,0:T(8,128)(2,1)S(1)} %get-tuple-element.64), channel_id=1, source_target_pairs={{0,3},{1,0},{2,1},{3,2},{4,7},{5,4},{6,5},{7,6},{8,11},{9,8},{10,9... | collective-permute-start | bytes 786440 | tf_op jit(solution)/shard_map/ppermute | solution.py:531
  55.4 9.6 %collective-permute-start.14 = (bf16[2,64,1024]{2,1,0:T(8,128)(2,1)S(1)}, bf16[2,64,1024]{2,1,0:T(8,128)(2,1)S(1)}, u32[]{:S(2)}, u32[]{:S(2)}) collective-permute-start(bf16[2,64,1024]{2,1,0:T(8,128)(2,1)S(1)} %get-tuple-element.65), channel_id=1, source_target_pairs={{0,2},{1,3},{2,0},{3,1},{4,6},{5,7},{6,4},{7,5},{8,10},{9,11},{10,... | collective-permute-start | bytes 786440 | tf_op jit(solution)/shard_map/ppermute | solution.py:531
  56.7 12.9 %collective-permute-start.15 = (bf16[2,64,1024]{2,1,0:T(8,128)(2,1)S(1)}, bf16[2,64,1024]{2,1,0:T(8,128)(2,1)S(1)}, u32[]{:S(2)}, u32[]{:S(2)}) collective-permute-start(bf16[2,64,1024]{2,1,0:T(8,128)(2,1)S(1)} %get-tuple-element.66), channel_id=1, source_target_pairs={{0,1},{1,2},{2,3},{3,0},{4,5},{5,6},{6,7},{7,4},{8,9},{9,10},{10,1... | collective-permute-start | bytes 786440 | tf_op jit(solution)/shard_map/ppermute | solution.py:531
